TPU v7x, 512 devices: a whole 4x8x8 slice. The times are simulated.
512 devices in a mesh: dp: 4 (over x), expert: 128 (over y, z, core).
Axes of the slice: x: 4, y: 8, z: 8, core: 2. Of those that a mesh axis runs over, the one named last changes fastest.
Arguments:
- tokens: bfloat16 [24576, 2560], P(('dp', 'expert')), may hold values from -6 to 6
- routes: int32 [4, 24576], P(None, ('dp', 'expert')), may hold values from 0 to 31, as said below
- counts: int32 [512, 128], P(('dp', 'expert')), may hold values from 0 to 2, as said below
- router: bfloat16 [2560, 128], P('dp'), may hold values from -0.125 to 0.125
- gate_up_weight: bfloat16 [128, 768, 2, 2560], P('expert', 'dp'), may hold values from -0.125 to 0.125
- down_weight: bfloat16 [128, 768, 2560], P('expert', 'dp'), may hold values from -0.21875 to 0.21875
- cotangent: bfloat16 [4, 24576, 2560], P(None, ('dp', 'expert')), may hold values from -6 to 6
Outputs:
- routed_out: bfloat16 [4, 24576, 2560], P(None, ('dp', 'expert'))
- token_grad: bfloat16 [24576, 2560], P(('dp', 'expert'))
- router_grad: float32 [2560, 128], P('dp', 'expert')
Inputs may be any that keep to these rules, and one draw needn't show every extreme that they name: `routes`: within the 48 tokens of one device, no expert of a member is named by more than 2 of that member's copies; in every draw one expert of each member is named by exactly 2 copies on every device. counts[b, m * 32 + l] is the number of tokens of device b (rows b * 48 to (b + 1) * 48 - 1) whose entry of routes for member m is l.
All inputs are finite; a program needn't handle non-finite values.
Results may differ from a plain program's by a relative error of at most 0.0064.
Values may be sent and summed in bfloat16 or wider, within the bound.
A program may use at most 64 MiB of HBM per device.

v0:
```python
import jax
import jax.numpy as jnp
from jax import lax
from jax.sharding import PartitionSpec as P

ROUTE_SCALE = 2.5
BALANCE = 1.0


def expert_pass(tok_rows, grad_rows, gate_weight, up_weight, down_weight):
    contract = (((1,), (1,)), ((), ()))
    gate_pre = lax.dot_general(tok_rows, gate_weight, contract, preferred_element_type=jnp.float32)
    up_pre = lax.dot_general(tok_rows, up_weight, contract, preferred_element_type=jnp.float32)
    squash = jax.nn.sigmoid(gate_pre)
    active = gate_pre * squash
    hidden = (active * up_pre).astype(jnp.bfloat16)
    expert_out = jnp.dot(hidden, down_weight, preferred_element_type=jnp.float32)
    hidden_grad = lax.dot_general(
        grad_rows, down_weight, contract, preferred_element_type=jnp.float32
    )
    gate_grad = (hidden_grad * up_pre * squash * (1.0 + gate_pre * (1.0 - squash))).astype(
        jnp.bfloat16
    )
    up_grad = (hidden_grad * active).astype(jnp.bfloat16)
    input_grad = jnp.dot(gate_grad, gate_weight, preferred_element_type=jnp.float32) + jnp.dot(
        up_grad, up_weight, preferred_element_type=jnp.float32
    )
    return (expert_out, input_grad)


def on_device(tokens, routes, counts, router, gate_up_weight, down_weight, cotangent):
    members, tok_local = routes.shape
    model_width = tokens.shape[1]
    experts = router.shape[1]
    per_member = experts // members
    capacity = max(2, tok_local // per_member + 1)
    slot_total = experts * capacity
    copy_count = members * tok_local
    tok_total = tok_local * lax.axis_size("dp") * lax.axis_size("expert")
    router_full = lax.all_gather(router, "dp", axis=0, tiled=True)
    logits = jnp.dot(tokens, router_full, preferred_element_type=jnp.float32)
    affinity = jax.nn.sigmoid(logits)
    owners = routes + per_member * jnp.arange(members, dtype=jnp.int32)[:, None]
    expert_ids = jnp.arange(experts, dtype=jnp.int32)
    chosen = (owners[:, :, None] == expert_ids[None, None, :]).astype(jnp.float32)
    gate_values = jnp.sum(chosen * affinity[None, :, :], axis=2)
    out_grad = (ROUTE_SCALE * gate_values[:, :, None] * cotangent.astype(jnp.float32)).astype(
        jnp.bfloat16
    )
    flat_owner = owners.reshape(copy_count)
    owner_hits = (flat_owner[:, None] == expert_ids[None, :]).astype(jnp.int32)
    rank_index = jnp.cumsum(owner_hits, axis=0) - 1
    slot_of = jnp.sum(owner_hits * rank_index, axis=1)
    target = flat_owner * capacity + slot_of
    placing = (jnp.arange(slot_total, dtype=jnp.int32)[:, None] == target[None, :]).astype(
        jnp.bfloat16
    )
    per_token = jnp.sum(placing.reshape(slot_total, members, tok_local), axis=1)
    send_tokens = (
        jnp.dot(per_token, tokens, preferred_element_type=jnp.float32)
        .astype(jnp.bfloat16)
        .reshape(experts, capacity, model_width)
    )
    send_grads = (
        jnp.dot(
            placing, out_grad.reshape(copy_count, model_width), preferred_element_type=jnp.float32
        )
        .astype(jnp.bfloat16)
        .reshape(experts, capacity, model_width)
    )
    recv_tokens, recv_grads = (
        lax.all_to_all(send_tokens, "expert", split_axis=0, concat_axis=0, tiled=True),
        lax.all_to_all(send_grads, "expert", split_axis=0, concat_axis=0, tiled=True),
    )
    tok_rows = recv_tokens.reshape(slot_total, model_width)
    grad_rows = recv_grads.reshape(slot_total, model_width)
    pair_piece = lax.all_gather(gate_up_weight, "dp", axis=1, tiled=True)
    down_piece = lax.all_gather(down_weight, "dp", axis=1, tiled=True)
    expert_out, input_grad = expert_pass(
        tok_rows, grad_rows, pair_piece[0, :, 0, :], pair_piece[0, :, 1, :], down_piece[0]
    )
    ret_out = expert_out.astype(jnp.bfloat16).reshape(experts, capacity, model_width)
    ret_grad = input_grad.astype(jnp.bfloat16).reshape(experts, capacity, model_width)
    back_out, back_grad = (
        lax.all_to_all(ret_out, "expert", split_axis=0, concat_axis=0, tiled=True),
        lax.all_to_all(ret_grad, "expert", split_axis=0, concat_axis=0, tiled=True),
    )
    first_axis = (((0,), (0,)), ((), ()))
    copy_out = (
        lax.dot_general(
            placing,
            back_out.reshape(slot_total, model_width),
            first_axis,
            preferred_element_type=jnp.float32,
        )
        .astype(jnp.bfloat16)
        .reshape(members, tok_local, model_width)
    )
    back_sum = lax.dot_general(
        per_token,
        back_grad.reshape(slot_total, model_width),
        first_axis,
        preferred_element_type=jnp.float32,
    )
    routed_out = (ROUTE_SCALE * gate_values[:, :, None] * copy_out.astype(jnp.float32)).astype(
        jnp.bfloat16
    )
    affinity_grad = ROUTE_SCALE * jnp.sum(
        cotangent.astype(jnp.float32) * copy_out.astype(jnp.float32), axis=2
    )
    expert_load = lax.psum(counts[0], ("dp", "expert"))
    balance = per_member * expert_load.astype(jnp.float32) / tok_total
    routed_grad = jnp.sum(chosen * affinity_grad[:, :, None], axis=0)
    logit_grad = (affinity * (1.0 - affinity) * (BALANCE * balance[None, :] + routed_grad)).astype(
        jnp.bfloat16
    )
    router_back = lax.dot_general(
        logit_grad, router_full, (((1,), (1,)), ((), ())), preferred_element_type=jnp.float32
    )
    token_grad = (back_sum + router_back).astype(jnp.bfloat16)
    partial_grad = lax.dot_general(
        tokens, logit_grad, first_axis, preferred_element_type=jnp.float32
    ) * tok_total ** (-0.5)
    column_share = lax.psum_scatter(partial_grad, "expert", scatter_dimension=1, tiled=True)
    router_grad = lax.psum_scatter(column_share, "dp", scatter_dimension=0, tiled=True)
    return (routed_out, token_grad, router_grad)


def solution(mesh):
    in_specs = (
        P(("dp", "expert"), None),
        P(None, ("dp", "expert")),
        P(("dp", "expert"), None),
        P("dp", None),
        P("expert", "dp", None, None),
        P("expert", "dp", None),
        P(None, ("dp", "expert"), None),
    )
    out_specs = (P(None, ("dp", "expert"), None), P(("dp", "expert"), None), P("dp", "expert"))
    return jax.shard_map(
        on_device, mesh=mesh, in_specs=in_specs, out_specs=out_specs, check_vma=False
    )
```

profile of v0, /device:TPU:1, one launch (start us, length us, event | category | flops | bytes accessed | tf_op | source)
XLA Modules:
  0.0 630.6 jit_solution(823001218682974081)
XLA Ops:
  7.2 3.2 copy.18
  10.5 0.7 all-gather.5.cloned.1.call-update
  11.3 0.1 reshape.84
  11.4 0.1 iota_compare_fusion.4
  11.5 0.1 fusion.24
  11.7 0.2 fusion.30
  11.9 0.1 reduce_sum.52
  12.1 0.1 fusion.28
  12.2 0.5 convolution_convert_fusion
  12.7 0.5 reshape.87
  13.3 53.8 %all_to_all.20 = bf16[128,2,2560]{2,1,0:T(2,128)(2,1)S(1)} all-to-all(bf16[128,2,2560]{2,1,0:T(2,128)(2,1)S(1)} %reshape.87), channel_id=1, replica_groups=mesh['dp'=4,'expert'=128] {'expert'}, dimensions={0} | all-to-all | bytes 2621440 | tf_op jit(solution)/shard_map/all_to_all | solution.py:72
  67.1 0.5 reshape.88
  67.6 32.6 %all-gather.3.cloned.1.call-done = bf16[1,768,2,2560]{3,1,2,0:T(8,128)(2,1)} async-done(((bf16[1,192,2,2560]{3,1,2,0:T(8,128)(2,1)}), bf16[1,768,2,2560]{3,1,2,0:T(8,128)(2,1)}) %all-gather.3.cloned.1.call-update) | async-done | bytes 7864336 | tf_op jit(solution)/shard_map/all_gather | solution.py:77
  100.2 4.4 fusion.11
  104.6 1.2 fusion.10
  105.8 48.9 %all-gather.5.cloned.1.call-done = bf16[1,768,2560]{2,1,0:T(8,128)(2,1)} async-done(((bf16[1,192,2560]{2,1,0:T(8,128)(2,1)}), bf16[1,768,2560]{2,1,0:T(8,128)(2,1)}) %all-gather.5.cloned.1.call-update) | async-done | bytes 3932176 | tf_op jit(solution)/shard_map/all_gather | solution.py:78
  154.7 3.6 fusion.4
  158.3 1.4 reshape.89
  159.7 14.4 %all-to-all-start.1 = ((bf16[128,2,2560]{2,1,0:T(2,128)(2,1)}), bf16[128,2,2560]{2,1,0:T(2,128)(2,1)S(1)}, u32[]{:S(2)}, u32[]{:S(2)}) async-start(bf16[128,2,2560]{2,1,0:T(2,128)(2,1)} %reshape.89), calls=%async_computation.1 | async-start | bytes 2621440 | tf_op jit(solution)/shard_map/all_to_all | solution.py:85
  174.1 11.0 %all_gather.9 = bf16[2560,128]{1,0:T(8,128)(2,1)S(1)} all-gather(bf16[640,128]{1,0:T(8,128)(2,1)S(1)} %copy-done.5), channel_id=1, replica_groups=mesh['dp'=4,'expert'=128] {'dp'}, dimensions={0}, use_global_device_ids=true | all-gather | bytes 819200 | tf_op jit(solution)/shard_map/all_gather | solution.py:40
  185.2 0.9 fusion.18
  186.0 23.6 %all-to-all-done.1 = bf16[128,2,2560]{2,1,0:T(2,128)(2,1)S(1)} async-done(((bf16[128,2,2560]{2,1,0:T(2,128)(2,1)}), bf16[128,2,2560]{2,1,0:T(2,128)(2,1)S(1)}, u32[]{:S(2)}, u32[]{:S(2)}) %all-to-all-start.1) | async-done | bytes 1310752 | tf_op jit(solution)/shard_map/all_to_all | solution.py:85
  209.7 0.5 reshape.90
  210.2 0.5 convolution_convert_fusion.2
  210.7 0.7 copy-done.1
  211.4 0.3 fusion.15
  211.8 0.8 select_reduce_fusion
  212.6 1.5 fusion.13
  214.0 0.5 convolution_convert_fusion.1
  214.5 0.5 reshape.92
  215.1 43.0 %all_to_all.21 = bf16[128,2,2560]{2,1,0:T(2,128)(2,1)S(1)} all-to-all(bf16[128,2,2560]{2,1,0:T(2,128)(2,1)S(1)} %reshape.92), channel_id=1, replica_groups=mesh['dp'=4,'expert'=128] {'expert'}, dimensions={0} | all-to-all | bytes 2621440 | tf_op jit(solution)/shard_map/all_to_all | solution.py:73
  258.0 0.5 reshape.93
  258.6 3.5 fusion
  262.1 3.6 fusion.9
  265.7 1.2 fusion.7
  266.9 1.4 reshape.94
  268.3 7.7 %all-to-all-start.3 = ((bf16[128,2,2560]{2,1,0:T(2,128)(2,1)}), bf16[128,2,2560]{2,1,0:T(2,128)(2,1)S(1)}, u32[]{:S(2)}, u32[]{:S(2)}) async-start(bf16[128,2,2560]{2,1,0:T(2,128)(2,1)} %reshape.94), calls=%async_computation.3 | async-start | bytes 2621440 | tf_op jit(solution)/shard_map/all_to_all | solution.py:86
  276.1 119.1 %psum.7 = s32[128]{0:T(128)S(1)} all-reduce(s32[128]{0:T(128)S(1)} %bitcast.57), channel_id=1, replica_groups=mesh['dp'=4,'expert'=128] {'dp','expert'}, use_global_device_ids=true, to_apply=%region_5.6 | all-reduce | flops 128 | bytes 1024 | tf_op jit(solution)/shard_map/psum | solution.py:111
  395.2 1.4 fusion.8
  396.7 1.3 dynamic-slice
  397.9 193.4 %all-reduce.4.cloned.1.call-done = f32[2560,128]{0,1:T(8,128)} async-done(((f32[2560,128]{0,1:T(8,128)}), f32[2560,128]{0,1:T(8,128)}) %all-reduce.4.cloned.1.call-update) | async-done | bytes 1310736
  591.4 1.5 constant_dynamic-slice_fusion
  592.9 1.5 copy.19
  594.5 1.1 fusion.36
  595.6 25.2 %reduce-scatter.4.cloned.1.call-done = f32[640,1]{1,0:T(8,128)} async-done(((f32[2560,1]{1,0:T(8,128)}), f32[640,1]{1,0:T(8,128)}) %reduce-scatter.4.cloned.1.call-update) | async-done | bytes 2576
  620.8 1.7 copy.20
  622.5 0.5 reshape.95
  623.1 1.0 fusion.12
  (53 shorter events, 0.6 us)
Async XLA Ops:
  7.2 5.0 copy-start
  7.2 93.0 %all-gather.3.cloned.1.call-start = ((), (), s32[]{:S(2)}) async-start(), calls=%async_computation.5 | async-start | bytes 9830400 | tf_op jit(solution)/shard_map/all_gather | solution.py:77
  10.4 0.8 copy-start.7
  10.5 144.2 %all-gather.5.cloned.1.call-start = ((), (), s32[]{:S(2)}) async-start(), calls=%async_computation.6 | async-start | bytes 4915200 | tf_op jit(solution)/shard_map/all_gather | solution.py:78
  100.2 4.4 copy-start.8
  105.8 52.5 %copy-start.10 = (f32[256,768]{1,0:T(8,128)}, f32[256,768]{1,0:T(8,128)S(1)}, u32[]{:S(2)}) copy-start(f32[256,768]{1,0:T(8,128)S(1)} %fusion.10) | copy-start | bytes 2359300
  159.7 14.4 %copy-start.5 = (bf16[640,128]{1,0:T(8,128)(2,1)S(1)}, bf16[640,128]{1,0:T(8,128)(2,1)}, u32[]{:S(2)}) copy-start(bf16[640,128]{1,0:T(8,128)(2,1)} %param.10) | copy-start | bytes 491524
  159.7 50.0 %all-to-all-start.1 = ((bf16[128,2,2560]{2,1,0:T(2,128)(2,1)}), bf16[128,2,2560]{2,1,0:T(2,128)(2,1)S(1)}, u32[]{:S(2)}, u32[]{:S(2)}) async-start(bf16[128,2,2560]{2,1,0:T(2,128)(2,1)} %reshape.89), calls=%async_computation.1 | async-start | bytes 2621440 | tf_op jit(solution)/shard_map/all_to_all | solution.py:85
  210.2 1.2 copy-start.1
  210.2 1.5 copy-start.3
  258.6 3.5 copy-start.11
  258.6 3.5 copy-start.12
  258.6 7.1 %slice-start = ((s8[7864320]{0:T(1024)(128)(4,1)}), s8[4194304]{0:T(1024)(128)(4,1)S(1)}, s32[]{:S(2)}) async-start(s8[7864320]{0:T(1024)(128)(4,1)} %bitcast.55), calls=%async_computation.9 | async-start | bytes 8388608
  262.1 3.6 slice-start.1
  268.3 7.8 %copy-start.9 = (s32[1,128]{1,0:T(1,128)S(1)}, s32[1,128]{1,0:T(1,128)}, u32[]{:S(2)}) copy-start(s32[1,128]{1,0:T(1,128)} %param.9) | copy-start | bytes 1540
  268.3 126.9 %copy-start.4 = (f32[48,128]{1,0:T(8,128)S(1)}, f32[48,128]{1,0:T(8,128)}, u32[]{:S(2)}) copy-start(f32[48,128]{1,0:T(8,128)} %fusion.18) | copy-start | bytes 73732
  268.3 126.9 %copy-start.6 = (f32[48,128]{1,0:T(8,128)S(1)}, f32[48,128]{1,0:T(8,128)}, u32[]{:S(2)}) copy-start(f32[48,128]{1,0:T(8,128)} %get-tuple-element.3) | copy-start | bytes 73732
  268.3 354.2 %all-to-all-start.3 = ((bf16[128,2,2560]{2,1,0:T(2,128)(2,1)}), bf16[128,2,2560]{2,1,0:T(2,128)(2,1)S(1)}, u32[]{:S(2)}, u32[]{:S(2)}) async-start(bf16[128,2,2560]{2,1,0:T(2,128)(2,1)} %reshape.94), calls=%async_computation.3 | async-start | bytes 2621440 | tf_op jit(solution)/shard_map/all_to_all | solution.py:86
  276.0 315.3 %all-reduce.4.cloned.1.call-start = ((), (), s32[]{:S(2)}) async-start(), calls=%async_computation.8 | async-start | bytes 2621440
  396.6 224.2 %reduce-scatter.4.cloned.1.call-start = ((), (), s32[]{:S(2)}) async-start(), calls=%async_computation.7 | async-start | bytes 1638400
  595.6 27.5 %copy-start.2 = (f32[48,2560]{1,0:T(8,128)S(1)}, f32[48,2560]{1,0:T(8,128)}, u32[]{:S(2)}) copy-start(f32[48,2560]{1,0:T(8,128)} %fusion.36) | copy-start | bytes 1474564
Sparse Core Ops, SparseCore 0:
  10.6 89.5 all-gather.2
  102.3 52.3 all-gather.4
  396.7 194.5 all-reduce.3
  594.6 26.2 reduce-scatter.3
where the time goes:
time: 632 us; the launch traced here: 631 us
  waiting for transfers between devices  325 us (51%)
  blocking collectives  227 us (36%)
  matrix products  23.4 us (4%)
  starting transfers between devices  22.3 us (4%)
  local copies, waits for them, and re-layouts  16.1 us (3%)
  between operations  14.1 us (2%)
    unnamed x6, waiting for transfers between devices  219 us
    psum x1, blocking collectives, on_device(): expert_load = lax.psum(counts[0], ('dp', 'expert'))  119 us
    all_to_all x1, blocking collectives, on_device(): lax.all_to_all(send_tokens, 'expert', split_axis=0, concat_axis=0, tiled=...  53.8 us
    all_gather x1, waiting for transfers between devices, on_device(): down_piece = lax.all_gather(down_weight, 'dp', axis=1, tiled=True)  48.9 us
    all_to_all x1, blocking collectives, on_device(): lax.all_to_all(send_grads, 'expert', split_axis=0, concat_axis=0, tiled=T...  43 us
    all_gather x1, waiting for transfers between devices, on_device(): pair_piece = lax.all_gather(gate_up_weight, 'dp', axis=1, tiled=True)  32.6 us
    all_to_all x1, waiting for transfers between devices, on_device(): lax.all_to_all(ret_out, 'expert', split_axis=0, concat_axis=0, tiled=True)  23.6 us
    all_to_all x1, starting transfers between devices, on_device(): lax.all_to_all(ret_out, 'expert', split_axis=0, concat_axis=0, tiled=True)  14.4 us
  transfers between devices with their start and end apart: 6, of which 5 were waited for; matrix products, arithmetic and copies ran while one was open for 3% of the time, Pallas kernels for 0%

commit v1 on v0

v1 whole, which is shorter than its diff:
```python
import functools

import jax
import jax.numpy as jnp
from jax import lax
from jax.experimental import pallas as pl
from jax.experimental.pallas import tpu as pltpu
from jax.sharding import PartitionSpec as P

ROUTE_SCALE = 2.5
BALANCE = 1.0
CAP = 2
STRIDE = 37
MESH = pl.DeviceIdType.MESH
BF16 = jnp.bfloat16
F32 = jnp.float32


def remote(src, dst, send_sem, recv_sem, device):
    return pltpu.make_async_remote_copy(
        src_ref=src,
        dst_ref=dst,
        send_sem=send_sem,
        recv_sem=recv_sem,
        device_id=device,
        device_id_type=MESH,
    )


def take_all(ref, count, sem):
    block = ref.at[pl.ds(0, count)]
    pltpu.make_async_copy(block, block, sem).wait()


def send_kernel(
    n_dp,
    n_exp,
    rows_ref,
    terms_ref,
    pair_ref,
    down_ref,
    rows_out,
    terms_out,
    pair_out,
    down_out,
    row_sems,
    term_sems,
    self_sems,
    own_send,
    own_recv,
    pass_send,
    pass_recv,
):
    d = lax.axis_index("dp")
    e = lax.axis_index("expert")
    sides = ((d + 1) % n_dp, (d + n_dp - 1) % n_dp)
    pair_step = pair_ref.shape[0] // 4
    down_step = down_ref.shape[0] // 2

    def piece(refs, shard, chunk):
        if chunk < 4:
            ref, part = refs[0], pl.ds(chunk * pair_step, pair_step)
        else:
            ref, part = refs[1], pl.ds((chunk - 4) * down_step, down_step)
        return ref.at[part] if shard is None else ref.at[shard, part]

    held = (pair_ref, down_ref)
    full = (pair_out, down_out)
    orders = ((0, 1, 2, 3, 4, 5), (3, 4, 5, 0, 1, 2))

    def own(side, chunk):
        return remote(
            piece(held, None, chunk),
            piece(full, d, chunk),
            own_send.at[side, chunk],
            own_recv.at[side, chunk],
            (sides[side], e),
        )

    def passed(side, chunk):
        source = sides[1 - side]
        return remote(
            piece(full, source, chunk),
            piece(full, source, chunk),
            pass_send.at[side, chunk % 3],
            pass_recv.at[side, chunk % 3],
            (sides[side], e),
        )

    for step in range(6):
        for side in range(2):
            own(side, orders[side][step]).start()
    locals_ = (
        pltpu.make_async_copy(pair_ref, pair_out.at[d], self_sems.at[0]),
        pltpu.make_async_copy(down_ref, down_out.at[d], self_sems.at[1]),
        pltpu.make_async_copy(rows_ref.at[e], rows_out.at[e], self_sems.at[2]),
        pltpu.make_async_copy(terms_ref.at[e], terms_out.at[e], self_sems.at[3]),
    )
    for copy in locals_:
        copy.start()

    def to_peer(s, carry):
        peer = (e + (s * STRIDE) % n_exp) % n_exp
        remote(
            rows_ref.at[peer], rows_out.at[e], row_sems.at[0], row_sems.at[1], (d, peer)
        ).start()
        remote(
            terms_ref.at[peer], terms_out.at[e], term_sems.at[0], term_sems.at[1], (d, peer)
        ).start()
        return carry

    lax.fori_loop(1, n_exp, to_peer, 0)

    for step in range(3):
        for side in range(2):
            chunk = orders[side][step]
            own(side, chunk).wait_recv()
            passed(side, chunk).start()
    for step in range(3, 6):
        for side in range(2):
            own(side, orders[side][step]).wait_recv()
    for copy in locals_:
        copy.wait()
    for step in range(6):
        for side in range(2):
            own(side, orders[side][step]).wait_send()
    for step in range(3):
        for side in range(2):
            passed(side, orders[side][step]).wait()
    take_all(rows_ref, n_exp - 1, row_sems.at[0])
    take_all(rows_out, n_exp - 1, row_sems.at[1])
    take_all(terms_ref, n_exp - 1, term_sems.at[0])
    take_all(terms_out, n_exp - 1, term_sems.at[1])


def return_kernel(
    n_dp, n_exp, rows_ref, sums_ref, rows_out, sums_out, row_sems, self_sems, sum_sems
):
    d = lax.axis_index("dp")
    e = lax.axis_index("expert")

    def small(step):
        peer = (d + step) % n_dp
        return remote(
            sums_ref.at[peer], sums_out.at[d], sum_sems.at[0, step], sum_sems.at[1, step], (peer, e)
        )

    for step in range(1, n_dp):
        small(step).start()
    locals_ = (
        pltpu.make_async_copy(rows_ref.at[e], rows_out.at[e], self_sems.at[0]),
        pltpu.make_async_copy(sums_ref.at[d], sums_out.at[d], self_sems.at[1]),
    )
    for copy in locals_:
        copy.start()

    def to_peer(s, carry):
        peer = (e + (s * STRIDE) % n_exp) % n_exp
        remote(
            rows_ref.at[peer], rows_out.at[e], row_sems.at[0], row_sems.at[1], (d, peer)
        ).start()
        return carry

    lax.fori_loop(1, n_exp, to_peer, 0)
    for copy in locals_:
        copy.wait()
    for step in range(1, n_dp):
        small(step).wait()
    take_all(rows_ref, n_exp - 1, row_sems.at[0])
    take_all(rows_out, n_exp - 1, row_sems.at[1])


def send_all(n_dp, n_exp, rows, terms, pair, down):
    def like(array):
        return jax.ShapeDtypeStruct(array.shape, array.dtype)

    def gathered(array):
        return jax.ShapeDtypeStruct((n_dp, *array.shape), array.dtype)

    dma = pltpu.SemaphoreType.DMA
    return pl.pallas_call(
        functools.partial(send_kernel, n_dp, n_exp),
        name="send_all",
        out_shape=(like(rows), like(terms), gathered(pair), gathered(down)),
        in_specs=[pl.BlockSpec(memory_space=pl.ANY)] * 4,
        out_specs=[pl.BlockSpec(memory_space=pl.ANY)] * 4,
        scratch_shapes=[
            dma((2,)),
            dma((2,)),
            dma((4,)),
            dma((2, 6)),
            dma((2, 6)),
            dma((2, 3)),
            dma((2, 3)),
        ],
        compiler_params=pltpu.CompilerParams(has_side_effects=True),
    )(rows, terms, pair, down)


def return_all(n_dp, n_exp, rows, sums):
    def like(array):
        return jax.ShapeDtypeStruct(array.shape, array.dtype)

    dma = pltpu.SemaphoreType.DMA
    return pl.pallas_call(
        functools.partial(return_kernel, n_dp, n_exp),
        name="return_all",
        out_shape=(like(rows), like(sums)),
        in_specs=[pl.BlockSpec(memory_space=pl.ANY)] * 2,
        out_specs=[pl.BlockSpec(memory_space=pl.ANY)] * 2,
        scratch_shapes=[dma((2,)), dma((2,)), dma((2, n_dp))],
        compiler_params=pltpu.CompilerParams(has_side_effects=True),
    )(rows, sums)


def expert_pass(tok_rows, grad_rows, gate_weight, up_weight, down_weight):
    contract = (((1,), (1,)), ((), ()))
    gate_pre = lax.dot_general(tok_rows, gate_weight, contract, preferred_element_type=F32)
    up_pre = lax.dot_general(tok_rows, up_weight, contract, preferred_element_type=F32)
    squash = jax.nn.sigmoid(gate_pre)
    active = gate_pre * squash
    hidden = (active * up_pre).astype(BF16)
    expert_out = jnp.dot(hidden, down_weight, preferred_element_type=F32)
    hidden_grad = lax.dot_general(grad_rows, down_weight, contract, preferred_element_type=F32)
    gate_grad = (hidden_grad * up_pre * squash * (1.0 + gate_pre * (1.0 - squash))).astype(BF16)
    up_grad = (hidden_grad * active).astype(BF16)
    input_grad = jnp.dot(gate_grad, gate_weight, preferred_element_type=F32) + jnp.dot(
        up_grad, up_weight, preferred_element_type=F32
    )
    return (expert_out, input_grad)


def on_device(n_dp, n_exp, tokens, routes, counts, router, gate_up_weight, down_weight, cotangent):
    members, tok_local = routes.shape
    width = tokens.shape[1]
    experts = router.shape[1]
    per_member = experts // members
    copies = members * tok_local
    tok_total = tok_local * n_dp * n_exp
    half = width // 2
    part = width // n_dp
    slots = experts * CAP
    mine = lax.axis_index("expert")

    router_full = lax.all_gather(router, "dp", axis=0, tiled=True)
    logits = jnp.dot(tokens, router_full, preferred_element_type=F32)
    affinity = jax.nn.sigmoid(logits)
    slope = affinity * (1.0 - affinity)
    dense = lax.dot_general(
        slope.astype(BF16), tokens, (((0,), (0,)), ((), ())), preferred_element_type=F32
    ).astype(BF16)
    spare = jnp.zeros((experts, experts), BF16)
    held = jnp.broadcast_to(counts.astype(BF16), (experts, experts))
    terms = jnp.concatenate([dense[:, :half], held, dense[:, half:], spare], axis=1)
    terms = terms.reshape(experts, 2, half + experts)

    earlier = (
        (routes[:, :, None] == routes[:, None, :])
        & (jnp.arange(tok_local)[None, None, :] < jnp.arange(tok_local)[None, :, None])
    ).astype(jnp.int32)
    rank = jnp.sum(earlier, axis=2)
    owners = routes + per_member * jnp.arange(members, dtype=jnp.int32)[:, None]
    first = owners * (2 * CAP) + rank
    row_ids = jnp.arange(2 * slots, dtype=jnp.int32)
    token_hits = jnp.any(row_ids[:, None, None] == first[None, :, :], axis=1)
    copy_hits = row_ids[:, None] == (first + CAP).reshape(1, copies)
    placing = jnp.concatenate([token_hits, copy_hits], axis=1).astype(BF16)
    stacked = jnp.concatenate([tokens, cotangent.reshape(copies, width)], axis=0)
    rows = (
        jnp.dot(placing, stacked, preferred_element_type=F32)
        .astype(BF16)
        .reshape(experts, 2 * CAP, width)
    )

    rows_in, terms_in, pair_full, down_full = send_all(
        n_dp, n_exp, rows, terms, gate_up_weight[0], down_weight[0]
    )

    tok_rows = rows_in[:, :CAP, :].reshape(slots, width)
    cot_rows = rows_in[:, CAP:, :].reshape(slots, width).astype(F32)
    row_logits = jnp.dot(tok_rows, router_full, preferred_element_type=F32)
    is_mine = (jnp.arange(experts, dtype=jnp.int32) == mine).astype(F32)
    gate = jax.nn.sigmoid(jnp.sum(row_logits * is_mine[None, :], axis=1, keepdims=True))
    router_column = jnp.sum(router_full.astype(F32) * is_mine[None, :], axis=1)
    grad_rows = (ROUTE_SCALE * gate * cot_rows).astype(BF16)
    pair = pair_full.reshape(-1, 2, width)
    expert_out, input_grad = expert_pass(
        tok_rows, grad_rows, pair[:, 0, :], pair[:, 1, :], down_full.reshape(-1, width)
    )
    expert_out = expert_out.astype(BF16).astype(F32)
    routed_rows = (ROUTE_SCALE * gate * expert_out).astype(BF16)
    affinity_grad = ROUTE_SCALE * jnp.sum(cot_rows * expert_out, axis=1, keepdims=True)
    lift = gate * (1.0 - gate) * affinity_grad
    back_rows = (input_grad + lift * router_column[None, :]).astype(BF16)
    routed_sum = lax.dot_general(
        lift.astype(BF16), tok_rows, (((0,), (0,)), ((), ())), preferred_element_type=F32
    )
    terms_sum = jnp.sum(terms_in.astype(F32), axis=0)
    dense_sum = terms_sum[:, :half].reshape(n_dp, part)
    load = jnp.broadcast_to(terms_sum[:1, half:], (n_dp, experts))
    sums = jnp.concatenate([dense_sum, routed_sum.reshape(n_dp, part), load], axis=1)
    short = -sums.shape[1] % 1024
    sums = jnp.pad(sums, ((0, 0), (0, short))).reshape(n_dp, 8, -1)
    results = jnp.concatenate(
        [back_rows.reshape(experts, CAP, width), routed_rows.reshape(experts, CAP, width)], axis=1
    )

    results_in, sums_in = return_all(n_dp, n_exp, results, sums)

    home = lax.dot_general(
        placing,
        results_in.reshape(2 * slots, width),
        (((0,), (0,)), ((), ())),
        preferred_element_type=F32,
    )
    total = jnp.sum(sums_in, axis=0).reshape(-1)
    balance = per_member * total[2 * part : 2 * part + experts] / tok_total
    router_grad = (
        BALANCE * jnp.sum(balance * is_mine) * total[:part] + total[part : 2 * part]
    ) * tok_total ** (-0.5)
    spread = (slope * (BALANCE * balance)[None, :]).astype(BF16)
    router_back = lax.dot_general(
        spread, router_full, (((1,), (1,)), ((), ())), preferred_element_type=F32
    )
    token_grad = (home[:tok_local] + router_back).astype(BF16)
    routed_out = home[tok_local:].astype(BF16).reshape(members, tok_local, width)
    return (routed_out, token_grad, router_grad[:, None])


def solution(mesh):
    in_specs = (
        P(("dp", "expert"), None),
        P(None, ("dp", "expert")),
        P(("dp", "expert"), None),
        P("dp", None),
        P("expert", "dp", None, None),
        P("expert", "dp", None),
        P(None, ("dp", "expert"), None),
    )
    out_specs = (P(None, ("dp", "expert"), None), P(("dp", "expert"), None), P("dp", "expert"))
    sizes = (mesh.shape["dp"], mesh.shape["expert"])
    return jax.shard_map(
        functools.partial(on_device, *sizes),
        mesh=mesh,
        in_specs=in_specs,
        out_specs=out_specs,
        check_vma=False,
    )
```

time: 632 us -> 313 us (0.50)
  waiting for transfers between devices: 325 us -> 0 us
  blocking collectives: 227 us -> 11.5 us
  Pallas kernels: 0 us -> 204 us
  local copies, waits for them, and re-layouts: 16.1 us -> 50.6 us
  starting transfers between devices: 22.3 us -> 0 us
  other arithmetic: 3.37 us -> 22.1 us
  between operations: 14.1 us -> 1.07 us
    unnamed x6 -> x0, waiting for transfers between devices: 219 us -> none
    pallas_call x0 -> x2, Pallas kernels: none -> 204 us  [the longest x1 120 us: send_all(): pl.pallas_call(functools.partial(send_kernel, n_dp, n_exp), name='send_al...]
    psum x1 -> x0, blocking collectives: 119 us -> none  [on_device(): expert_load = lax.psum(counts[0], ('dp', 'expert'))]
    all_to_all x2 -> x0, blocking collectives: 96.7 us -> none  [the longest x1 53.8 us: on_device(): lax.all_to_all(send_tokens, 'expert', split_axis=0, concat_axis=0, tiled=...]
    all_gather x2 -> x0, waiting for transfers between devices: 81.5 us -> none  [the longest x1 48.9 us: on_device(): down_piece = lax.all_gather(down_weight, 'dp', axis=1, tiled=True)]
    all_to_all x2 -> x0, waiting for transfers between devices: 23.6 us -> none  [the longest x1 23.6 us: on_device(): lax.all_to_all(ret_out, 'expert', split_axis=0, concat_axis=0, tiled=True)]
    all_to_all x2 -> x0, starting transfers between devices: 22.1 us -> none  [the longest x1 14.4 us: on_device(): lax.all_to_all(ret_out, 'expert', split_axis=0, concat_axis=0, tiled=True)]
    slice x0 -> x4, local copies, waits for them, and re-layouts: none -> 18.2 us  [the longest x1 15.5 us: on_device(): pair[:, 0, :]]
  transfers between devices with their start and end apart: 6 -> 0, of which waited for: 5 -> 0; matrix products, arithmetic and copies ran while one was open for 3% -> 0% of each run, Pallas kernels for 0% -> 0%
where the time goes in v1:
time: 313 us
  Pallas kernels  204 us (65%)
  local copies, waits for them, and re-layouts  50.6 us (16%)
  matrix products  23.5 us (8%)
  other arithmetic  22.1 us (7%)
  blocking collectives  11.5 us (4%)
    pallas_call x1, Pallas kernels, send_all(): pl.pallas_call(functools.partial(send_kernel, n_dp, n_exp), name='send_al...  120 us
    pallas_call x1, Pallas kernels, return_all(): pl.pallas_call(functools.partial(return_kernel, n_dp, n_exp), name='retur...  84.1 us
    slice x1, local copies, waits for them, and re-layouts, on_device(): pair[:, 0, :]  15.5 us
    all_gather x1, blocking collectives, on_device(): router_full = lax.all_gather(router, 'dp', axis=0, tiled=True)  11.5 us
    unnamed x36, local copies, waits for them, and re-layouts  6.9 us

profile of v1, /device:TPU:1, one launch (start us, length us, event | category | flops | bytes accessed | tf_op | source)
XLA Modules:
  0.0 312.8 jit_solution(8903758302157713747)
XLA Ops:
  0.7 0.7 convert_bitcast_fusion
  1.4 1.0 convert_reduce_fusion.1
  2.4 0.8 broadcast_add_fusion
  3.2 0.1 fusion.19
  3.4 0.8 copy.12
  4.1 0.7 iota_compare_fusion
  4.9 11.5 %all_gather.3 = bf16[2560,128]{1,0:T(8,128)(2,1)S(1)} all-gather(bf16[640,128]{1,0:T(8,128)(2,1)} %param.10), channel_id=1, replica_groups=mesh['dp'=4,'expert'=128] {'dp'}, dimensions={0}, use_global_device_ids=true | all-gather | bytes 819200 | tf_op jit(solution)/shard_map/all_gather | solution.py:245
  16.4 1.0 multiply_reduce_fusion.1
  17.4 1.2 subtract_multiply_fusion
  18.6 0.4 convolution_convert_fusion.2
  19.0 0.2 maximum_maximum_fusion
  19.2 1.0 reshape.127.terms_ref
  20.2 2.2 convolution_convert_fusion
  22.4 2.3 reshape.126.rows_ref
  24.7 120.0 %send_all.1 = (bf16[128,4,2560]{2,1,0:T(4,128)(2,1)}, bf16[128,2,1408]{2,1,0:T(2,128)(2,1)}, bf16[4,192,2,2560]{3,2,1,0:T(2,128)(2,1)}, bf16[4,192,2560]{2,1,0:T(8,128)(2,1)}) custom-call(bf16[128,4,2560]{2,1,0:T(4,128)(2,1)} %reshape.126.rows_ref, bf16[128,2,1408]{2,1,0:T(2,128)(2,1)} %reshape.127.terms_ref, bf16[192,2,2560]{2,1,0:T(2,128)(2,1)} %bitcast.51, ...), custom_call_target="tpu_custom_call" | custom-call | tf_op jit(solution)/shard_map/send_all/pallas_call | solution.py:181
  144.7 1.7 convert_reduce_fusion
  146.5 6.0 %slice_convert_fusion.1 = (f32[128,2,2560]{2,1,0:T(2,128)S(1)}, bf16[128,2,2560]{2,1,0:T(2,128)(2,1)}) fusion(bf16[128,4,2560]{2,1,0:T(4,128)(2,1)} %get-tuple-element.9), kind=kLoop, calls=%fused_computation.24 | loop fusion | flops 655360 | bytes 6553600 | tf_op jit(solution)/shard_map/convert_element_type | solution.py:280
  152.5 2.9 reshape.140
  155.4 3.2 %reshape.128 = bf16[256,2560]{1,0:T(8,128)(2,1)S(1)} reshape(bf16[128,2,2560]{2,1,0:T(2,128)(2,1)} %get-tuple-element.23) | data formatting | bytes 2621440 | tf_op jit(solution)/shard_map/reshape | solution.py:279
  158.6 0.6 fusion.13
  159.2 15.5 %fusion.36 = (bf16[768,1,2560]{2,1,0:T(2,128)(2,1)S(1)}, bf16[768,1,2560]{2,1,0:T(2,128)(2,1)S(1)}) fusion(bf16[768,2,2560]{2,1,0:T(2,128)(2,1)} %bitcast.45), kind=kLoop, calls=%fused_computation.78 | loop fusion | bytes 15728640 | tf_op jit(solution)/shard_map/slice | solution.py:288
  174.7 3.0 copy-done.2
  177.8 1.2 fusion.6
  179.0 1.2 copy-done.1
  180.2 1.2 fusion.4
  181.4 0.8 copy-done
  182.2 1.2 copy-done.5
  183.4 1.3 multiply_reduce_fusion
  184.8 0.3 fusion.7
  185.1 1.3 multiply_convert_fusion
  186.4 4.0 %reshape.132 = bf16[128,2,2560]{2,1,0:T(2,128)(2,1)} reshape(bf16[256,2560]{1,0:T(8,128)(2,1)} %multiply_convert_fusion) | data formatting | bytes 2621440 | tf_op jit(solution)/shard_map/reshape | solution.py:305
  190.3 0.6 copy.34
  191.0 0.1 reshape.139
  191.1 3.1 multiply_convert_fusion.1
  194.2 3.2 %convert_element_type.88 = bf16[256,2560]{1,0:T(8,128)(2,1)S(1)} reshape(bf16[128,2,2560]{2,1,0:T(2,128)(2,1)} %multiply_convert_fusion.1) | data formatting | bytes 2621440 | tf_op jit(solution)/shard_map/convert_element_type | solution.py:285
  197.4 3.5 %fusion.38 = f32[256,768]{1,0:T(8,128)S(1)} fusion(bf16[256,2560]{1,0:T(8,128)(2,1)S(1)} %convert_element_type.88, bf16[768,2560]{1,0:T(8,128)(2,1)} %bitcast.49), kind=kOutput, calls=%fused_computation.80 | convolution fusion | flops 1006632960 | bytes 6029312 | tf_op jit(solution)/shard_map/dot_general | solution.py:224
  200.9 4.8 %fusion.5 = f32[256,2560]{1,0:T(8,128)S(1)} fusion(bf16[768,1,2560]{2,1,0:T(2,128)(2,1)} %copy-done.2, f32[256,768]{1,0:T(8,128)S(1)} %copy-done.9, f32[256,768]{1,0:T(8,128)S(1)} %fusion.38, f32[256,768]{1,0:T(8,128)S(1)} %copy-done.11), kind=kOutput, calls=%fused_computation.17 | convolution fusion | flops 1008599040 | bytes 8912896 | tf_op jit(solution)/shard_map/dot_general | solution.py:227
  205.7 2.5 fusion.2
  208.2 3.2 %reshape.131 = bf16[128,2,2560]{2,1,0:T(2,128)(2,1)S(1)} reshape(bf16[256,2560]{1,0:T(8,128)(2,1)} %fusion.2) | data formatting | bytes 2621440 | tf_op jit(solution)/shard_map/reshape | solution.py:305
  211.4 4.2 %pad_maximum_fusion.rows_ref = bf16[128,4,2560]{2,1,0:T(4,128)(2,1)} fusion(bf16[128,2,2560]{2,1,0:T(2,128)(2,1)S(1)} %copy-done.4, bf16[128,2,2560]{2,1,0:T(2,128)(2,1)S(1)} %reshape.131), kind=kLoop, calls=%fused_computation.11 | loop fusion | flops 5242880 | bytes 5242880 | tf_op jit(solution)/shard_map/concatenate | solution.py:304
  215.6 84.1 %return_all.1 = (bf16[128,4,2560]{2,1,0:T(4,128)(2,1)}, f32[4,8,256]{2,1,0:T(8,128)}) custom-call(bf16[128,4,2560]{2,1,0:T(4,128)(2,1)} %pad_maximum_fusion.rows_ref, f32[4,8,256]{2,1,0:T(8,128)} %bitcast.56), custom_call_target="tpu_custom_call" | custom-call | tf_op jit(solution)/shard_map/return_all/pallas_call | solution.py:205
  299.7 4.2 %reshape.135 = bf16[512,2560]{1,0:T(8,128)(2,1)S(1)} reshape(bf16[128,4,2560]{2,1,0:T(4,128)(2,1)} %get-tuple-element.13) | data formatting | bytes 5242880 | tf_op jit(solution)/shard_map/reshape | solution.py:312
  303.9 2.4 fusion.22
  306.3 0.6 fusion.27
  306.9 0.6 fusion.25
  307.6 0.6 broadcast_in_dim.17
  308.2 2.1 fusion.3
  310.2 2.6 slice.79
  (51 shorter events, 0.3 us)
Async XLA Ops:
  0.6 18.0 %copy-start.6 = (bf16[48,2560]{1,0:T(8,128)(2,1)S(1)}, bf16[48,2560]{1,0:T(8,128)(2,1)}, u32[]{:S(2)}) copy-start(bf16[48,2560]{1,0:T(8,128)(2,1)} %param.7) | copy-start | bytes 737284
  174.7 3.1 copy-start.2
  174.7 5.5 %copy-start.1 = (bf16[768,1,2560]{2,1,0:T(2,128)(2,1)}, bf16[768,1,2560]{2,1,0:T(2,128)(2,1)S(1)}, u32[]{:S(2)}) copy-start(bf16[768,1,2560]{2,1,0:T(2,128)(2,1)S(1)} %get-tuple-element.21) | copy-start | bytes 11796484
  180.2 1.2 copy-start.8
  180.2 2.0 copy-start
  180.2 3.2 %copy-start.5 = (bf16[4,192,2560]{2,1,0:T(8,128)(2,1)S(1)}, bf16[4,192,2560]{2,1,0:T(8,128)(2,1)}, u32[]{:S(2)}) copy-start(bf16[4,192,2560]{2,1,0:T(8,128)(2,1)} %get-tuple-element.10) | copy-start | bytes 11796484
  183.4 1.3 copy-start.10
  185.1 6.0 %copy-start.3 = (bf16[128,4,2560]{2,1,0:T(4,128)(2,1)S(1)}, bf16[128,4,2560]{2,1,0:T(4,128)(2,1)}, u32[]{:S(2)}) copy-start(bf16[128,4,2560]{2,1,0:T(4,128)(2,1)} %get-tuple-element.9) | copy-start | bytes 7864324
  197.4 3.5 %copy-start.9 = (f32[256,768]{1,0:T(8,128)S(1)}, f32[256,768]{1,0:T(8,128)}, u32[]{:S(2)}) copy-start(f32[256,768]{1,0:T(8,128)} %copy-done.8) | copy-start | bytes 2359300
  197.4 3.5 %copy-start.11 = (f32[256,768]{1,0:T(8,128)S(1)}, f32[256,768]{1,0:T(8,128)}, u32[]{:S(2)}) copy-start(f32[256,768]{1,0:T(8,128)} %copy-done.10) | copy-start | bytes 2359300
  197.4 8.3 %slice-start = ((s8[7864320]{0:T(1024)(128)(4,1)}), s8[4194304]{0:T(1024)(128)(4,1)S(1)}, s32[]{:S(2)}) async-start(s8[7864320]{0:T(1024)(128)(4,1)} %bitcast.47), calls=%async_computation | async-start | bytes 8388608
  200.9 4.8 %slice-start.1 = ((s8[7864320]{0:T(1024)(128)(4,1)}), s8[3670016]{0:T(1024)(128)(4,1)S(1)}, s32[]{:S(2)}) async-start(s8[7864320]{0:T(1024)(128)(4,1)} %bitcast.47), calls=%async_computation.1 | async-start | bytes 7340032
  200.9 4.8 %copy-start.14 = (f32[2560]{0:T(1024)S(1)}, f32[2560]{0:T(1024)}, u32[]{:S(2)}) copy-start(f32[2560]{0:T(1024)} %multiply_reduce_fusion.1) | copy-start | bytes 30724
  208.2 3.2 %copy-start.4 = (bf16[128,2,2560]{2,1,0:T(2,128)(2,1)S(1)}, bf16[128,2,2560]{2,1,0:T(2,128)(2,1)}, u32[]{:S(2)}) copy-start(bf16[128,2,2560]{2,1,0:T(2,128)(2,1)} %reshape.132) | copy-start | bytes 3932164
  299.7 4.2 %copy-start.7 = (pred[512,192]{1,0:T(32,128)(4,1)S(1)}, pred[512,192]{1,0:T(32,128)(4,1)}, u32[]{:S(2)}) copy-start(pred[512,192]{1,0:T(32,128)(4,1)} %iota_compare_fusion) | copy-start | bytes 294916
  299.7 4.2 %copy-start.12 = (pred[512,48]{1,0:T(32,128)(4,1)S(1)}, pred[512,48]{1,0:T(32,128)(4,1)}, u32[]{:S(2)}) copy-start(pred[512,48]{1,0:T(32,128)(4,1)} %copy.12) | copy-start | bytes 73732
  303.9 2.4 copy-start.13

commit v2 on v1

--- a/solution.py
+++ b/solution.py
@@ -2,6 +2,7 @@
 
 import jax
 import jax.numpy as jnp
+import numpy as np
 from jax import lax
 from jax.experimental import pallas as pl
 from jax.experimental.pallas import tpu as pltpu
@@ -37,11 +38,13 @@
     n_exp,
     rows_ref,
     terms_ref,
-    pair_ref,
+    gate_ref,
+    up_ref,
     down_ref,
     rows_out,
     terms_out,
-    pair_out,
+    gate_out,
+    up_out,
     down_out,
     row_sems,
     term_sems,
@@ -54,18 +57,14 @@
     d = lax.axis_index("dp")
     e = lax.axis_index("expert")
     sides = ((d + 1) % n_dp, (d + n_dp - 1) % n_dp)
-    pair_step = pair_ref.shape[0] // 4
-    down_step = down_ref.shape[0] // 2
+    span = gate_ref.shape[0] // 2
+    held = (gate_ref, up_ref, down_ref)
+    full = (gate_out, up_out, down_out)
 
     def piece(refs, shard, chunk):
-        if chunk < 4:
-            ref, part = refs[0], pl.ds(chunk * pair_step, pair_step)
-        else:
-            ref, part = refs[1], pl.ds((chunk - 4) * down_step, down_step)
+        ref, part = refs[chunk // 2], pl.ds(chunk % 2 * span, span)
         return ref.at[part] if shard is None else ref.at[shard, part]
 
-    held = (pair_ref, down_ref)
-    full = (pair_out, down_out)
     orders = ((0, 1, 2, 3, 4, 5), (3, 4, 5, 0, 1, 2))
 
     def own(side, chunk):
@@ -91,8 +90,9 @@
         for side in range(2):
             own(side, orders[side][step]).start()
     locals_ = (
-        pltpu.make_async_copy(pair_ref, pair_out.at[d], self_sems.at[0]),
-        pltpu.make_async_copy(down_ref, down_out.at[d], self_sems.at[1]),
+        pltpu.make_async_copy(gate_ref, gate_out.at[d], self_sems.at[0]),
+        pltpu.make_async_copy(up_ref, up_out.at[d], self_sems.at[1]),
+        pltpu.make_async_copy(down_ref, down_out.at[d], self_sems.at[4]),
         pltpu.make_async_copy(rows_ref.at[e], rows_out.at[e], self_sems.at[2]),
         pltpu.make_async_copy(terms_ref.at[e], terms_out.at[e], self_sems.at[3]),
     )
@@ -170,7 +170,7 @@
     take_all(rows_out, n_exp - 1, row_sems.at[1])
 
 
-def send_all(n_dp, n_exp, rows, terms, pair, down):
+def send_all(n_dp, n_exp, rows, terms, gate, up, down):
     def like(array):
         return jax.ShapeDtypeStruct(array.shape, array.dtype)
 
@@ -181,20 +181,20 @@
     return pl.pallas_call(
         functools.partial(send_kernel, n_dp, n_exp),
         name="send_all",
-        out_shape=(like(rows), like(terms), gathered(pair), gathered(down)),
-        in_specs=[pl.BlockSpec(memory_space=pl.ANY)] * 4,
-        out_specs=[pl.BlockSpec(memory_space=pl.ANY)] * 4,
+        out_shape=(like(rows), like(terms), gathered(gate), gathered(up), gathered(down)),
+        in_specs=[pl.BlockSpec(memory_space=pl.ANY)] * 5,
+        out_specs=[pl.BlockSpec(memory_space=pl.ANY)] * 5,
         scratch_shapes=[
             dma((2,)),
             dma((2,)),
-            dma((4,)),
+            dma((5,)),
             dma((2, 6)),
             dma((2, 6)),
             dma((2, 3)),
             dma((2, 3)),
         ],
         compiler_params=pltpu.CompilerParams(has_side_effects=True),
-    )(rows, terms, pair, down)
+    )(rows, terms, gate, up, down)
 
 
 def return_all(n_dp, n_exp, rows, sums):
@@ -213,21 +213,197 @@
     )(rows, sums)
 
 
-def expert_pass(tok_rows, grad_rows, gate_weight, up_weight, down_weight):
-    contract = (((1,), (1,)), ((), ()))
-    gate_pre = lax.dot_general(tok_rows, gate_weight, contract, preferred_element_type=F32)
-    up_pre = lax.dot_general(tok_rows, up_weight, contract, preferred_element_type=F32)
+def arrange(group):
+    i = np.arange(group * 16)
+    quarter, kind, expert, slot = i // (4 * group), i // (2 * group) % 2, i // 2 % group, i % 2
+    move = np.zeros((group * 16, group * 16), np.float32)
+    move[i, expert * 16 + quarter * 4 + kind * 2 + slot] = 1.0
+    return move
+
+
+def pack(first, second, unmove, quarter):
+    parts = []
+    for q in range(4):
+        columns = slice(q * quarter, (q + 1) * quarter)
+        parts += [first[:, columns], second[:, columns]]
+    stacked = jnp.concatenate(parts, axis=0)
+    return jnp.dot(unmove, stacked, preferred_element_type=F32).astype(BF16)
+
+
+def pack_kernel(placing_ref, stacked_ref, unmove_ref, out_ref):
+    rows = jnp.dot(placing_ref[...], stacked_ref[...], preferred_element_type=F32).astype(BF16)
+    half = rows.shape[0] // 2
+    out_ref[...] = pack(rows[:half], rows[half:], unmove_ref[...], out_ref.shape[1])
+
+
+def pack_rows(group, placing, stacked, unmove):
+    count, width = placing.shape[0], stacked.shape[1]
+    return pl.pallas_call(
+        pack_kernel,
+        name="pack_rows",
+        grid=(count // (4 * group),),
+        out_shape=jax.ShapeDtypeStruct((count * 4, width // 4), BF16),
+        in_specs=[
+            pl.BlockSpec((4 * group, stacked.shape[0]), lambda i: (i, 0)),
+            pl.BlockSpec(stacked.shape, lambda i: (0, 0)),
+            pl.BlockSpec(unmove.shape, lambda i: (0, 0)),
+        ],
+        out_specs=pl.BlockSpec((16 * group, width // 4), lambda i: (i, 0)),
+        compiler_params=pltpu.CompilerParams(vmem_limit_bytes=32 << 20),
+    )(placing, stacked, unmove)
+
+
+def expert_kernel(
+    group,
+    rows_ref,
+    move_ref,
+    unmove_ref,
+    router_ref,
+    mine_ref,
+    gate_ref,
+    up_ref,
+    down_ref,
+    out_ref,
+    sum_ref,
+    tok,
+    cot,
+    grad,
+    value,
+    total_out,
+    total_grad,
+):
+    step = pl.program_id(0)
+    quarter = rows_ref.shape[1]
+    block, span = 16 * group, 2 * group
+    blocks = rows_ref.shape[0] // block
+    transposed = (((1,), (1,)), ((), ()))
+
+    @pl.when(step == 0)
+    def _():
+        for b in range(blocks):
+            moved = jnp.dot(
+                move_ref[...], rows_ref[pl.ds(b * block, block), :], preferred_element_type=F32
+            ).astype(BF16)
+            for q in range(4):
+                at = (pl.ds(b * span, span), pl.ds(q * quarter, quarter))
+                tok[at] = moved[2 * q * span : (2 * q + 1) * span]
+                cot[at] = moved[(2 * q + 1) * span : (2 * q + 2) * span]
+        logits = jnp.dot(tok[...], router_ref[...], preferred_element_type=F32)
+        gate = jax.nn.sigmoid(jnp.sum(logits * mine_ref[0:1, :], axis=1, keepdims=True))
+        value[...] = jnp.broadcast_to(gate, value.shape)
+        grad[...] = (ROUTE_SCALE * gate * cot[...].astype(F32)).astype(BF16)
+
+    gate_pre = lax.dot_general(tok[...], gate_ref[...], transposed, preferred_element_type=F32)
+    up_pre = lax.dot_general(tok[...], up_ref[...], transposed, preferred_element_type=F32)
+    hidden_grad = lax.dot_general(
+        grad[...], down_ref[...], transposed, preferred_element_type=F32
+    )
     squash = jax.nn.sigmoid(gate_pre)
     active = gate_pre * squash
     hidden = (active * up_pre).astype(BF16)
-    expert_out = jnp.dot(hidden, down_weight, preferred_element_type=F32)
-    hidden_grad = lax.dot_general(grad_rows, down_weight, contract, preferred_element_type=F32)
     gate_grad = (hidden_grad * up_pre * squash * (1.0 + gate_pre * (1.0 - squash))).astype(BF16)
     up_grad = (hidden_grad * active).astype(BF16)
-    input_grad = jnp.dot(gate_grad, gate_weight, preferred_element_type=F32) + jnp.dot(
-        up_grad, up_weight, preferred_element_type=F32
-    )
-    return (expert_out, input_grad)
+    more_out = jnp.dot(hidden, down_ref[...], preferred_element_type=F32)
+    more_grad = jnp.dot(gate_grad, gate_ref[...], preferred_element_type=F32) + jnp.dot(
+        up_grad, up_ref[...], preferred_element_type=F32
+    )
+
+    @pl.when(step == 0)
+    def _():
+        total_out[...] = more_out
+        total_grad[...] = more_grad
+
+    @pl.when(step > 0)
+    def _():
+        total_out[...] += more_out
+        total_grad[...] += more_grad
+
+    @pl.when(step == pl.num_programs(0) - 1)
+    def _():
+        gate = value[:, 0:1]
+        expert_out = total_out[...].astype(BF16).astype(F32)
+        affinity_grad = ROUTE_SCALE * jnp.sum(
+            cot[...].astype(F32) * expert_out, axis=1, keepdims=True
+        )
+        lift = gate * (1.0 - gate) * affinity_grad
+        column = lax.dot_general(
+            mine_ref[...].astype(BF16), router_ref[...], transposed, preferred_element_type=F32
+        )[0:1]
+        sum_ref[...] = jnp.broadcast_to(
+            jnp.sum(lift * tok[...].astype(F32), axis=0, keepdims=True), sum_ref.shape
+        )
+        grad[...] = (total_grad[...] + lift * column).astype(BF16)
+        tok[...] = (ROUTE_SCALE * gate * expert_out).astype(BF16)
+        for b in range(blocks):
+            at = pl.ds(b * span, span)
+            out_ref[pl.ds(b * block, block), :] = pack(
+                grad[at, :], tok[at, :], unmove_ref[...], quarter
+            )
+
+
+def expert_rows(group, rows, move, unmove, router, mine, gate, up, down):
+    hidden, width = gate.shape
+    tile = 256
+    slots = rows.shape[0] // 8
+
+    def whole(array):
+        return pl.BlockSpec(array.shape, lambda i: (0,) * array.ndim)
+
+    weight = pl.BlockSpec((tile, width), lambda i: (i, 0))
+    summed = jax.ShapeDtypeStruct((8, width), F32)
+    return pl.pallas_call(
+        functools.partial(expert_kernel, group),
+        name="expert_rows",
+        grid=(hidden // tile,),
+        out_shape=(jax.ShapeDtypeStruct(rows.shape, BF16), summed),
+        in_specs=[whole(rows), whole(move), whole(unmove), whole(router), whole(mine)]
+        + [weight] * 3,
+        out_specs=(whole(rows), whole(summed)),
+        scratch_shapes=[
+            pltpu.VMEM((slots, width), BF16),
+            pltpu.VMEM((slots, width), BF16),
+            pltpu.VMEM((slots, width), BF16),
+            pltpu.VMEM((slots, 128), F32),
+            pltpu.VMEM((slots, width), F32),
+            pltpu.VMEM((slots, width), F32),
+        ],
+        compiler_params=pltpu.CompilerParams(vmem_limit_bytes=58 << 20),
+    )(rows, move, unmove, router, mine, gate, up, down)
+
+
+def home_kernel(group, rows_ref, move_ref, taking_ref, spread_ref, router_ref, routed_ref, token_ref, flat):
+    quarter = rows_ref.shape[1]
+    block, part = 16 * group, 4 * group
+    for b in range(rows_ref.shape[0] // block):
+        moved = jnp.dot(
+            move_ref[...], rows_ref[pl.ds(b * block, block), :], preferred_element_type=F32
+        ).astype(BF16)
+        for q in range(4):
+            flat[pl.ds(b * part, part), pl.ds(q * quarter, quarter)] = moved[
+                q * part : (q + 1) * part
+            ]
+    home = jnp.dot(taking_ref[...], flat[...], preferred_element_type=F32)
+    back = lax.dot_general(
+        spread_ref[...], router_ref[...], (((1,), (1,)), ((), ())), preferred_element_type=F32
+    )
+    tokens = token_ref.shape[0]
+    token_ref[...] = (home[:tokens] + back).astype(BF16)
+    routed_ref[...] = home[tokens:].astype(BF16)
+
+
+def home_rows(group, rows, move, taking, spread, router):
+    tokens, width = spread.shape[0], router.shape[0]
+
+    def out(count):
+        return jax.ShapeDtypeStruct((count, width), BF16)
+
+    return pl.pallas_call(
+        functools.partial(home_kernel, group),
+        name="home_rows",
+        out_shape=(out(taking.shape[0] - tokens), out(tokens)),
+        scratch_shapes=[pltpu.VMEM((rows.shape[0] // 4, width), BF16)],
+        compiler_params=pltpu.CompilerParams(vmem_limit_bytes=32 << 20),
+    )(rows, move, taking, spread, router)
 
 
 def on_device(n_dp, n_exp, tokens, routes, counts, router, gate_up_weight, down_weight, cotangent):
@@ -260,70 +436,69 @@
     ).astype(jnp.int32)
     rank = jnp.sum(earlier, axis=2)
     owners = routes + per_member * jnp.arange(members, dtype=jnp.int32)[:, None]
-    first = owners * (2 * CAP) + rank
+    group = min(16, experts)
+    move_np = arrange(group)
+    move, unmove = jnp.asarray(move_np, BF16), jnp.asarray(move_np.T, BF16)
+    first = owners // group * (4 * group) + owners % group * CAP + rank
+    second = first + 2 * group
     row_ids = jnp.arange(2 * slots, dtype=jnp.int32)
     token_hits = jnp.any(row_ids[:, None, None] == first[None, :, :], axis=1)
-    copy_hits = row_ids[:, None] == (first + CAP).reshape(1, copies)
+    copy_hits = row_ids[:, None] == second.reshape(1, copies)
     placing = jnp.concatenate([token_hits, copy_hits], axis=1).astype(BF16)
+    token_takes = jnp.any(first[:, :, None] == row_ids[None, None, :], axis=0)
+    copy_takes = second.reshape(copies, 1) == row_ids[None, :]
+    taking = jnp.concatenate([token_takes, copy_takes], axis=0).astype(BF16)
     stacked = jnp.concatenate([tokens, cotangent.reshape(copies, width)], axis=0)
-    rows = (
-        jnp.dot(placing, stacked, preferred_element_type=F32)
-        .astype(BF16)
-        .reshape(experts, 2 * CAP, width)
-    )
-
-    rows_in, terms_in, pair_full, down_full = send_all(
-        n_dp, n_exp, rows, terms, gate_up_weight[0], down_weight[0]
-    )
-
-    tok_rows = rows_in[:, :CAP, :].reshape(slots, width)
-    cot_rows = rows_in[:, CAP:, :].reshape(slots, width).astype(F32)
-    row_logits = jnp.dot(tok_rows, router_full, preferred_element_type=F32)
+    rows = pack_rows(group, placing, stacked, unmove).reshape(experts, 16, width // 4)
+
+    rows_in, terms_in, gate_full, up_full, down_full = send_all(
+        n_dp,
+        n_exp,
+        rows,
+        terms,
+        gate_up_weight[0, :, 0, :],
+        gate_up_weight[0, :, 1, :],
+        down_weight[0],
+    )
+
     is_mine = (jnp.arange(experts, dtype=jnp.int32) == mine).astype(F32)
-    gate = jax.nn.sigmoid(jnp.sum(row_logits * is_mine[None, :], axis=1, keepdims=True))
-    router_column = jnp.sum(router_full.astype(F32) * is_mine[None, :], axis=1)
-    grad_rows = (ROUTE_SCALE * gate * cot_rows).astype(BF16)
-    pair = pair_full.reshape(-1, 2, width)
-    expert_out, input_grad = expert_pass(
-        tok_rows, grad_rows, pair[:, 0, :], pair[:, 1, :], down_full.reshape(-1, width)
-    )
-    expert_out = expert_out.astype(BF16).astype(F32)
-    routed_rows = (ROUTE_SCALE * gate * expert_out).astype(BF16)
-    affinity_grad = ROUTE_SCALE * jnp.sum(cot_rows * expert_out, axis=1, keepdims=True)
-    lift = gate * (1.0 - gate) * affinity_grad
-    back_rows = (input_grad + lift * router_column[None, :]).astype(BF16)
-    routed_sum = lax.dot_general(
-        lift.astype(BF16), tok_rows, (((0,), (0,)), ((), ())), preferred_element_type=F32
+    results, routed_sum = expert_rows(
+        group,
+        rows_in.reshape(experts * 16, width // 4),
+        move,
+        unmove,
+        router_full,
+        jnp.broadcast_to(is_mine[None, :], (8, experts)),
+        gate_full.reshape(-1, width),
+        up_full.reshape(-1, width),
+        down_full.reshape(-1, width),
     )
     terms_sum = jnp.sum(terms_in.astype(F32), axis=0)
     dense_sum = terms_sum[:, :half].reshape(n_dp, part)
     load = jnp.broadcast_to(terms_sum[:1, half:], (n_dp, experts))
-    sums = jnp.concatenate([dense_sum, routed_sum.reshape(n_dp, part), load], axis=1)
+    sums = jnp.concatenate([dense_sum, routed_sum[0].reshape(n_dp, part), load], axis=1)
     short = -sums.shape[1] % 1024
     sums = jnp.pad(sums, ((0, 0), (0, short))).reshape(n_dp, 8, -1)
-    results = jnp.concatenate(
-        [back_rows.reshape(experts, CAP, width), routed_rows.reshape(experts, CAP, width)], axis=1
-    )
-
-    results_in, sums_in = return_all(n_dp, n_exp, results, sums)
-
-    home = lax.dot_general(
-        placing,
-        results_in.reshape(2 * slots, width),
-        (((0,), (0,)), ((), ())),
-        preferred_element_type=F32,
-    )
+
+    results_in, sums_in = return_all(
+        n_dp, n_exp, results.reshape(experts, 16, width // 4), sums
+    )
+
     total = jnp.sum(sums_in, axis=0).reshape(-1)
     balance = per_member * total[2 * part : 2 * part + experts] / tok_total
     router_grad = (
         BALANCE * jnp.sum(balance * is_mine) * total[:part] + total[part : 2 * part]
     ) * tok_total ** (-0.5)
     spread = (slope * (BALANCE * balance)[None, :]).astype(BF16)
-    router_back = lax.dot_general(
-        spread, router_full, (((1,), (1,)), ((), ())), preferred_element_type=F32
-    )
-    token_grad = (home[:tok_local] + router_back).astype(BF16)
-    routed_out = home[tok_local:].astype(BF16).reshape(members, tok_local, width)
+    routed_out, token_grad = home_rows(
+        group,
+        results_in.reshape(experts * 16, width // 4),
+        move,
+        taking,
+        spread,
+        router_full,
+    )
+    routed_out = routed_out.reshape(members, tok_local, width)
     return (routed_out, token_grad, router_grad[:, None])
 
 

time: 313 us -> 258 us (0.82)
  local copies, waits for them, and re-layouts: 50.6 us -> 10.2 us
  Pallas kernels: 204 us -> 228 us
  matrix products: 23.5 us -> 2.72 us
  other arithmetic: 22.1 us -> 3.9 us
    pallas_call x0 -> x3, Pallas kernels: none -> 24.3 us  [the longest x1 17 us: expert_rows(): pl.pallas_call(functools.partial(expert_kernel, group), name='expert_rows...]
    dot_general x11 -> x0, matrix products: 22 us -> none  [the longest x1 4.77 us: expert_pass(): jnp.dot(gate_grad, gate_weight, preferred_element_type=F32)]
    reshape x5 -> x0, local copies, waits for them, and re-layouts: 16.8 us -> none  [the longest x1 4.16 us: on_device(): results_in.reshape(2 * slots, width)]
    slice x2, local copies, waits for them, and re-layouts: 18.1 us -> 3.72 us  [the longest x1 2.8 us: on_device(): gate_up_weight[0, :, 1, :]]
    convert_element_type x4 -> x3, other arithmetic: 10.4 us -> 0.23 us  [the longest x1 0.21 us: on_device(): placing = jnp.concatenate([token_hits, copy_hits], axis=1).astype(BF16)]
    convert_element_type x3 -> x0, local copies, waits for them, and re-layouts: 6.06 us -> none  [the longest x1 3.18 us: on_device(): grad_rows = (ROUTE_SCALE * gate * cot_rows).astype(BF16)]
    unnamed x36 -> x26, local copies, waits for them, and re-layouts: 6.9 us -> 2.42 us
    concatenate x2, other arithmetic: 4.22 us -> 0.09 us  [the longest x1 0.08 us: on_device(): jnp.concatenate([tokens, cotangent.reshape(copies, width)], axis=0)]
where the time goes in v2:
time: 258 us
  Pallas kernels  228 us (88%)
  blocking collectives  11.5 us (4%)
  local copies, waits for them, and re-layouts  10.2 us (4%)
  other arithmetic  3.9 us (2%)
  matrix products  2.72 us (1%)
    pallas_call x1, Pallas kernels, send_all(): pl.pallas_call(functools.partial(send_kernel, n_dp, n_exp), name='send_al...  120 us
    pallas_call x1, Pallas kernels, return_all(): pl.pallas_call(functools.partial(return_kernel, n_dp, n_exp), name='retur...  84 us
    pallas_call x1, Pallas kernels, expert_rows(): pl.pallas_call(functools.partial(expert_kernel, group), name='expert_rows...  17 us
    all_gather x1, blocking collectives, on_device(): router_full = lax.all_gather(router, 'dp', axis=0, tiled=True)  11.5 us

profile of v2, /device:TPU:1, one launch (start us, length us, event | category | flops | bytes accessed | tf_op | source)
XLA Modules:
  0.0 257.7 jit_solution(6570566515543907724)
XLA Ops:
  0.6 0.0 copy-start.11
  0.6 11.5 %all_gather.3.router_ref = bf16[2560,128]{1,0:T(8,128)(2,1)S(1)} all-gather(bf16[640,128]{1,0:T(8,128)(2,1)} %param.12), channel_id=1, replica_groups=mesh['dp'=4,'expert'=128] {'dp'}, dimensions={0}, use_global_device_ids=true | all-gather | bytes 819200 | tf_op jit(solution)/shard_map/all_gather | solution.py:421
  12.2 1.4 subtract_multiply_fusion
  13.6 1.3 convolution_convert_fusion
  14.9 0.0 copy-start.10
  15.0 0.0 copy-start.7
  15.0 0.0 copy-start.8
  15.0 0.0 copy-done.11
  15.1 0.2 maximum_maximum_fusion
  15.2 0.0 copy-done
  15.3 0.0 copy-start.5
  15.3 1.0 reshape.81.terms_ref
  16.3 0.0 copy-done.10
  16.3 0.2 convert_reduce_fusion.1
  16.5 0.1 broadcast_add_fusion
  16.6 0.1 eq.86
  16.7 0.1 iota_compare_fusion
  16.8 0.1 fusion.3
  16.9 0.2 copy.14
  17.1 0.2 add_convert_fusion.placing_ref
  17.3 0.0 copy-done.7
  17.3 0.0 copy-done.8
  17.3 0.1 pad_maximum_fusion.stacked_ref
  17.4 0.0 copy-start.6
  17.4 4.6 %pack_rows.1 = bf16[2048,640]{1,0:T(8,128)(2,1)S(1)} custom-call(bf16[512,240]{1,0:T(8,128)(2,1)S(1)} %add_convert_fusion.placing_ref, bf16[240,2560]{1,0:T(8,128)(2,1)S(1)} %pad_maximum_fusion.stacked_ref, bf16[256,256]{1,0:T(8,128)(2,1)S(1)} %copy-done.5), custom_call_target="tpu_custom_call" | custom-call | tf_op jit(solution)/shard_map/pack_rows/pallas_call | solution.py:241
  22.1 0.0 copy-start.2
  22.1 0.0 copy-done.6
  22.1 2.8 %fusion.15 = (bf16[1,192,1,2560]{3,2,1,0:T(2,128)(2,1)S(1)}, bf16[1,192,1,2560]{3,2,1,0:T(2,128)(2,1)S(1)}) fusion(bf16[1,192,2,2560]{3,2,1,0:T(2,128)(2,1)S(1)} %copy-done.6), kind=kLoop, calls=%fused_computation.49 | loop fusion | bytes 3932160 | tf_op jit(solution)/shard_map/slice | solution.py:460
  24.9 0.0 copy-done.2
  24.9 1.5 copy_bitcast_fusion
  26.4 120.0 %send_all.1 = (bf16[128,16,640]{2,1,0:T(8,128)(2,1)}, bf16[128,2,1408]{2,1,0:T(2,128)(2,1)}, bf16[4,192,2560]{2,1,0:T(8,128)(2,1)}, bf16[4,192,2560]{2,1,0:T(8,128)(2,1)}, bf16[4,192,2560]{2,1,0:T(8,128)(2,1)}) custom-call(bf16[128,16,640]{2,1,0:T(8,128)(2,1)} %bitcast.27, bf16[128,2,1408]{2,1,0:T(2,128)(2,1)} %reshape.81.terms_ref, ...), custom_call_target="tpu_custom_call" | custom-call | tf_op jit(solution)/shard_map/send_all/pallas_call | solution.py:181
  146.5 0.6 broadcast_in_dim.17.mine_ref
  147.1 17.0 %expert_rows.1 = (bf16[2048,640]{1,0:T(8,128)(2,1)}, f32[8,2560]{1,0:T(8,128)}) custom-call(bf16[2048,640]{1,0:T(8,128)(2,1)} %bitcast.33, bf16[256,256]{1,0:T(8,128)(2,1)} %constant.61.clone.move_ref, bf16[256,256]{1,0:T(8,128)(2,1)} %constant.62.clone.unmove_ref, bf16[2560,128]{1,0:T(8,128)(2,1)} %copy-done, f32[8,128]{1,0:T(8,128)} %broadcast_in_dim.17.mine_ref, ...), custom_call_target="tpu_custom_call" | custom-call | tf_op jit(solution)/shard_map/expert_rows/pallas_call | solution.py:354
  164.1 0.9 slice_reduce_fusion
  165.0 0.0 copy-done.9
  165.0 0.0 copy-start.1
  165.0 0.0 copy-start.4
  165.0 0.6 convert_reduce_fusion
  165.7 0.6 copy.24
  166.4 84.0 %return_all.1 = (bf16[128,16,640]{2,1,0:T(8,128)(2,1)}, f32[4,8,256]{2,1,0:T(8,128)}) custom-call(bf16[128,16,640]{2,1,0:T(8,128)(2,1)} %bitcast.32, f32[4,8,256]{2,1,0:T(8,128)} %bitcast.37), custom_call_target="tpu_custom_call" | custom-call | tf_op jit(solution)/shard_map/return_all/pallas_call | solution.py:205
  250.4 0.8 reduce_sum.38
  251.2 0.6 fusion.13
  251.8 0.6 fusion.6
  252.4 0.6 broadcast_in_dim.20
  253.0 0.1 iota_compare_fusion.1
  253.2 0.1 fusion.4
  253.3 1.7 copy-done.3
  255.1 2.7 %home_rows.1 = (bf16[192,2560]{1,0:T(8,128)(2,1)}, bf16[48,2560]{1,0:T(8,128)(2,1)}) custom-call(bf16[2048,640]{1,0:T(8,128)(2,1)S(1)} %bitcast.28, bf16[256,256]{1,0:T(8,128)(2,1)S(1)} %copy-done.4, bf16[240,512]{1,0:T(8,128)(2,1)S(1)} %add_convert_fusion.1.taking_ref, bf16[48,128]{1,0:T(8,128)(2,1)S(1)} %multiply_convert_fusion.spread_ref, ...), custom_call_target="tpu_custom_call" | custom-call | tf_op jit(solution)/shard_map/home_rows/pallas_call | solution.py:400
  (24 shorter events, 0.2 us)
Async XLA Ops:
  0.6 14.4 %copy-start.11 = (s32[1,128]{1,0:T(1,128)S(1)}, s32[1,128]{1,0:T(1,128)}, u32[]{:S(2)}) copy-start(s32[1,128]{1,0:T(1,128)} %param.11) | copy-start | bytes 1540
  12.2 3.1 %copy-start = (bf16[2560,128]{1,0:T(8,128)(2,1)}, bf16[2560,128]{1,0:T(8,128)(2,1)S(1)}, u32[]{:S(2)}) copy-start(bf16[2560,128]{1,0:T(8,128)(2,1)S(1)} %all_gather.3.router_ref) | copy-start | bytes 1966084
  14.9 1.4 copy-start.10
  15.0 2.3 copy-start.7
  15.0 2.3 copy-start.8
  15.3 2.2 copy-start.5
  17.4 4.6 %copy-start.6 = (bf16[1,192,2,2560]{3,2,1,0:T(2,128)(2,1)S(1)}, bf16[1,192,2,2560]{3,2,1,0:T(2,128)(2,1)}, u32[]{:S(2)}) copy-start(bf16[1,192,2,2560]{3,2,1,0:T(2,128)(2,1)} %param.13) | copy-start | bytes 5898244
  22.1 2.8 %copy-start.2 = (bf16[2048,640]{1,0:T(8,128)(2,1)}, bf16[2048,640]{1,0:T(8,128)(2,1)S(1)}, u32[]{:S(2)}) copy-start(bf16[2048,640]{1,0:T(8,128)(2,1)S(1)} %pack_rows.1) | copy-start | bytes 7864324
  147.1 17.9 %copy-start.9 = (bf16[128,2,1408]{2,1,0:T(2,128)(2,1)S(1)}, bf16[128,2,1408]{2,1,0:T(2,128)(2,1)}, u32[]{:S(2)}) copy-start(bf16[128,2,1408]{2,1,0:T(2,128)(2,1)} %get-tuple-element.19) | copy-start | bytes 2162692
  165.0 88.3 %copy-start.1 = (bf16[2560,128]{1,0:T(8,128)(2,1)S(1)}, bf16[2560,128]{1,0:T(8,128)(2,1)}, u32[]{:S(2)}) copy-start(bf16[2560,128]{1,0:T(8,128)(2,1)} %copy-done) | copy-start | bytes 1966084
  165.0 88.3 %copy-start.4 = (bf16[256,256]{1,0:T(8,128)(2,1)S(1)}, bf16[256,256]{1,0:T(8,128)(2,1)}, u32[]{:S(2)}) copy-start(bf16[256,256]{1,0:T(8,128)(2,1)} %constant.61.clone.move_ref) | copy-start | bytes 393220
  253.3 1.7 copy-start.3

commit v3 on v2

v3 whole, which is shorter than its diff:
```python
import functools

import jax
import jax.numpy as jnp
import numpy as np
from jax import lax
from jax.experimental import pallas as pl
from jax.experimental.pallas import tpu as pltpu
from jax.sharding import PartitionSpec as P

ROUTE_SCALE = 2.5
BALANCE = 1.0
CAP = 2
STRIDE = 37
MESH = pl.DeviceIdType.MESH
BF16 = jnp.bfloat16
F32 = jnp.float32


def remote(src, dst, send_sem, recv_sem, device):
    return pltpu.make_async_remote_copy(
        src_ref=src,
        dst_ref=dst,
        send_sem=send_sem,
        recv_sem=recv_sem,
        device_id=device,
        device_id_type=MESH,
    )


def take_all(ref, count, sem):
    block = ref.at[pl.ds(0, count)]
    pltpu.make_async_copy(block, block, sem).wait()


def send_rows(n_exp, d, e, source, target, sems):
    def to_peer(s, carry):
        peer = (e + (s * STRIDE) % n_exp) % n_exp
        remote(source.at[peer], target.at[e], sems.at[0], sems.at[1], (d, peer)).start()
        return carry

    lax.fori_loop(1, n_exp, to_peer, 0)


def send_kernel(
    n_dp,
    n_exp,
    placing_ref,
    stacked_ref,
    unmove_ref,
    unterm_ref,
    counts_ref,
    router_ref,
    gate_ref,
    up_ref,
    down_ref,
    rows_out,
    terms_out,
    router_out,
    slope_out,
    gate_out,
    up_out,
    down_out,
    rows,
    terms,
    router_all,
    row_sems,
    term_sems,
    self_sems,
    half_sems,
    swap_sems,
    own_send,
    own_recv,
    pass_send,
    pass_recv,
):
    d = lax.axis_index("dp")
    e = lax.axis_index("expert")
    core = e % 2
    sibling = e + 1 - 2 * core
    sides = ((d + 1) % n_dp, (d + n_dp - 1) % n_dp)
    span = gate_ref.shape[0] // 2
    held = (gate_ref, up_ref, down_ref)
    full = (gate_out, up_out, down_out)

    def piece(refs, shard, chunk):
        ref, part = refs[chunk // 2], pl.ds(chunk % 2 * span, span)
        return ref.at[part] if shard is None else ref.at[shard, part]

    orders = ((0, 1, 2, 3, 4, 5), (3, 4, 5, 0, 1, 2))

    def own(side, chunk):
        return remote(
            piece(held, None, chunk),
            piece(full, d, chunk),
            own_send.at[side, chunk],
            own_recv.at[side, chunk],
            (sides[side], e),
        )

    def passed(side, chunk):
        source = sides[1 - side]
        return remote(
            piece(full, source, chunk),
            piece(full, source, chunk),
            pass_send.at[side, chunk % 3],
            pass_recv.at[side, chunk % 3],
            (sides[side], e),
        )

    def router_half(step):
        return remote(
            router_ref.at[core],
            router_all.at[d, core],
            half_sems.at[0, step],
            half_sems.at[1, step],
            ((d + step) % n_dp, e),
        )

    def router_swap(step):
        shard = (d + n_dp - step) % n_dp
        return remote(
            router_all.at[shard, core],
            router_all.at[shard, core],
            swap_sems.at[0, step],
            swap_sems.at[1, step],
            (d, sibling),
        )

    for step in range(1, n_dp):
        router_half(step).start()
    for step in range(6):
        for side in range(2):
            own(side, orders[side][step]).start()
    own_router = pltpu.make_async_copy(router_ref, router_all.at[d], self_sems.at[5])
    own_router.start()
    locals_ = [
        pltpu.make_async_copy(gate_ref, gate_out.at[d], self_sems.at[0]),
        pltpu.make_async_copy(up_ref, up_out.at[d], self_sems.at[1]),
        pltpu.make_async_copy(down_ref, down_out.at[d], self_sems.at[2]),
    ]
    for copy in locals_:
        copy.start()

    group = unmove_ref.shape[0] // 16
    quarter = rows.shape[2]
    for b in range(n_exp // group):
        placed = jnp.dot(
            placing_ref[pl.ds(b * 4 * group, 4 * group), :],
            stacked_ref[...],
            preferred_element_type=F32,
        ).astype(BF16)
        rows[pl.ds(b * group, group)] = pack(
            placed[: 2 * group], placed[2 * group :], unmove_ref[...], quarter
        ).reshape(group, 16, quarter)
    send_rows(n_exp, d, e, rows, rows_out, row_sems)
    locals_.append(pltpu.make_async_copy(rows.at[e], rows_out.at[e], self_sems.at[3]))
    locals_[-1].start()

    for step in range(1, n_dp):
        router_half(step).wait_recv()
        router_swap(step).start()
    own_router.wait()
    for step in range(1, n_dp):
        router_swap(step).wait_recv()
    router = router_all[...].reshape(router_out.shape)
    router_out[...] = router
    tokens = stacked_ref[pl.ds(0, slope_out.shape[0]), :]
    affinity = jax.nn.sigmoid(jnp.dot(tokens, router, preferred_element_type=F32))
    slope = affinity * (1.0 - affinity)
    slope_out[...] = slope
    dense = lax.dot_general(
        slope.astype(BF16), tokens, (((0,), (0,)), ((), ())), preferred_element_type=F32
    ).astype(BF16)
    lanes = terms.shape[2]
    parts = tokens.shape[1] // lanes
    blank = jnp.zeros(((15 - parts) * group, lanes), BF16)
    for b in range(n_exp // group):
        block = [
            dense[b * group : (b + 1) * group, r * lanes : (r + 1) * lanes] for r in range(parts)
        ]
        stack = jnp.concatenate([*block, counts_ref[...], blank], axis=0)
        moved = jnp.dot(unterm_ref[...], stack, preferred_element_type=F32).astype(BF16)
        terms[pl.ds(b * group, group)] = moved.reshape(group, 16, lanes)
    send_rows(n_exp, d, e, terms, terms_out, term_sems)
    locals_.append(pltpu.make_async_copy(terms.at[e], terms_out.at[e], self_sems.at[4]))
    locals_[-1].start()

    for step in range(3):
        for side in range(2):
            chunk = orders[side][step]
            own(side, chunk).wait_recv()
            passed(side, chunk).start()
    for step in range(3, 6):
        for side in range(2):
            own(side, orders[side][step]).wait_recv()
    for copy in locals_:
        copy.wait()
    for step in range(1, n_dp):
        router_half(step).wait_send()
        router_swap(step).wait_send()
    for step in range(6):
        for side in range(2):
            own(side, orders[side][step]).wait_send()
    for step in range(3):
        for side in range(2):
            passed(side, orders[side][step]).wait()
    take_all(rows, n_exp - 1, row_sems.at[0])
    take_all(rows_out, n_exp - 1, row_sems.at[1])
    take_all(terms, n_exp - 1, term_sems.at[0])
    take_all(terms_out, n_exp - 1, term_sems.at[1])


def send_all(n_dp, n_exp, tokens, placing, stacked, unmove, unterm, counts, router, gate, up, down):
    width = stacked.shape[1]
    experts = placing.shape[0] // 4

    def gathered(array):
        return jax.ShapeDtypeStruct((n_dp, *array.shape), array.dtype)

    dma = pltpu.SemaphoreType.DMA
    hbm, vmem = pl.BlockSpec(memory_space=pl.ANY), pl.BlockSpec(memory_space=pltpu.VMEM)
    rows = (experts, 16, width // 4)
    terms = (experts, 16, 256)
    return pl.pallas_call(
        functools.partial(send_kernel, n_dp, n_exp),
        name="send_all",
        out_shape=(
            jax.ShapeDtypeStruct(rows, BF16),
            jax.ShapeDtypeStruct(terms, BF16),
            jax.ShapeDtypeStruct((width, experts), BF16),
            jax.ShapeDtypeStruct((tokens, experts), F32),
            gathered(gate),
            gathered(up),
            gathered(down),
        ),
        in_specs=[vmem] * 6 + [hbm] * 3,
        out_specs=[hbm, hbm, vmem, vmem, hbm, hbm, hbm],
        scratch_shapes=[
            pltpu.VMEM(rows, BF16),
            pltpu.VMEM(terms, BF16),
            pltpu.VMEM((n_dp, *router.shape), BF16),
            dma((2,)),
            dma((2,)),
            dma((6,)),
            dma((2, n_dp)),
            dma((2, n_dp)),
            dma((2, 6)),
            dma((2, 6)),
            dma((2, 3)),
            dma((2, 3)),
        ],
        compiler_params=pltpu.CompilerParams(
            has_side_effects=True, vmem_limit_bytes=40 << 20
        ),
    )(placing, stacked, unmove, unterm, counts, router, gate, up, down)


def arrange(group):
    i = np.arange(group * 16)
    quarter, kind, expert, slot = i // (4 * group), i // (2 * group) % 2, i // 2 % group, i % 2
    move = np.zeros((group * 16, group * 16), np.float32)
    move[i, expert * 16 + quarter * 4 + kind * 2 + slot] = 1.0
    return move


def arrange_terms(group):
    i = np.arange(group * 16)
    move = np.zeros((group * 16, group * 16), np.float32)
    move[i, i % 16 * group + i // 16] = 1.0
    return move


def pack(first, second, unmove, quarter):
    parts = []
    for q in range(4):
        columns = slice(q * quarter, (q + 1) * quarter)
        parts += [first[:, columns], second[:, columns]]
    stacked = jnp.concatenate(parts, axis=0)
    return jnp.dot(unmove, stacked, preferred_element_type=F32).astype(BF16)


def expert_kernel(
    n_dp,
    n_exp,
    group,
    per_token,
    rows_ref,
    move_ref,
    unmove_ref,
    router_ref,
    mine_ref,
    terms_ref,
    slope_ref,
    taking_ref,
    gate_ref,
    up_ref,
    down_ref,
    routed_ref,
    token_ref,
    dense_ref,
    sum_ref,
    tok,
    cot,
    grad,
    value,
    total_out,
    total_grad,
    back,
    land,
    flat,
    dense,
    dense_land,
    lifted,
    lifted_land,
    row_sems,
    self_sems,
    dense_sems,
    lifted_sems,
):
    d = lax.axis_index("dp")
    e = lax.axis_index("expert")
    step = pl.program_id(0)
    quarter = rows_ref.shape[1]
    block, span = 16 * group, 2 * group
    blocks = rows_ref.shape[0] // block
    transposed = (((1,), (1,)), ((), ()))

    @pl.when(step == 0)
    def _():
        for b in range(blocks):
            moved = jnp.dot(
                move_ref[...], rows_ref[pl.ds(b * block, block), :], preferred_element_type=F32
            ).astype(BF16)
            for q in range(4):
                at = (pl.ds(b * span, span), pl.ds(q * quarter, quarter))
                tok[at] = moved[2 * q * span : (2 * q + 1) * span]
                cot[at] = moved[(2 * q + 1) * span : (2 * q + 2) * span]
        logits = jnp.dot(tok[...], router_ref[...], preferred_element_type=F32)
        gate = jax.nn.sigmoid(jnp.sum(logits * mine_ref[0:1, :], axis=1, keepdims=True))
        value[...] = jnp.broadcast_to(gate, value.shape)
        grad[...] = (ROUTE_SCALE * gate * cot[...].astype(F32)).astype(BF16)

    gate_pre = lax.dot_general(tok[...], gate_ref[...], transposed, preferred_element_type=F32)
    up_pre = lax.dot_general(tok[...], up_ref[...], transposed, preferred_element_type=F32)
    hidden_grad = lax.dot_general(
        grad[...], down_ref[...], transposed, preferred_element_type=F32
    )
    squash = jax.nn.sigmoid(gate_pre)
    active = gate_pre * squash
    hidden = (active * up_pre).astype(BF16)
    gate_grad = (hidden_grad * up_pre * squash * (1.0 + gate_pre * (1.0 - squash))).astype(BF16)
    up_grad = (hidden_grad * active).astype(BF16)
    more_out = jnp.dot(hidden, down_ref[...], preferred_element_type=F32)
    more_grad = jnp.dot(gate_grad, gate_ref[...], preferred_element_type=F32) + jnp.dot(
        up_grad, up_ref[...], preferred_element_type=F32
    )

    @pl.when(step == 0)
    def _():
        total_out[...] = more_out
        total_grad[...] = more_grad

    @pl.when(step > 0)
    def _():
        total_out[...] += more_out
        total_grad[...] += more_grad

    @pl.when(step == pl.num_programs(0) - 1)
    def _():
        gate = value[:, 0:1]
        expert_out = total_out[...].astype(BF16).astype(F32)
        affinity_grad = ROUTE_SCALE * jnp.sum(
            cot[...].astype(F32) * expert_out, axis=1, keepdims=True
        )
        lift = gate * (1.0 - gate) * affinity_grad
        column = lax.dot_general(
            mine_ref[...].astype(BF16), router_ref[...], transposed, preferred_element_type=F32
        )[0:1]
        lifted[...] = jnp.broadcast_to(
            jnp.sum(lift * tok[...].astype(F32), axis=0, keepdims=True), lifted.shape
        )
        dense[...] = jnp.sum(terms_ref[...].astype(F32), axis=0)

        def small(shift, ref, target, sems):
            return remote(
                ref,
                target.at[d],
                sems.at[0, shift],
                sems.at[1, shift],
                ((d + shift) % n_dp, e),
            )

        smalls = []
        for shift in range(1, n_dp):
            smalls.append(small(shift, dense, dense_land, dense_sems))
            smalls.append(small(shift, lifted, lifted_land, lifted_sems))
        for copy in smalls:
            copy.start()
        grad[...] = (total_grad[...] + lift * column).astype(BF16)
        tok[...] = (ROUTE_SCALE * gate * expert_out).astype(BF16)
        for b in range(blocks):
            at = pl.ds(b * span, span)
            back[pl.ds(b * group, group)] = pack(
                grad[at, :], tok[at, :], unmove_ref[...], quarter
            ).reshape(group, 16, quarter)
        send_rows(n_exp, d, e, back, land, row_sems)
        locals_ = (
            pltpu.make_async_copy(back.at[e], land.at[e], self_sems.at[0]),
            pltpu.make_async_copy(dense, dense_land.at[d], self_sems.at[1]),
            pltpu.make_async_copy(lifted, lifted_land.at[d], self_sems.at[2]),
        )
        for copy in locals_:
            copy.start()
        for copy in locals_:
            copy.wait()
        for copy in smalls:
            copy.wait()
        sum_ref[...] = jnp.sum(lifted_land[...], axis=0)
        all_dense = jnp.sum(dense_land[...], axis=0)
        dense_ref[...] = all_dense
        parts = tok.shape[1] // all_dense.shape[1]
        load = all_dense[parts : parts + 1, : slope_ref.shape[1]]
        spread = (slope_ref[...] * (BALANCE * (per_token * load))).astype(BF16)
        router_back = lax.dot_general(
            spread, router_ref[...], transposed, preferred_element_type=F32
        )

        take_all(back, n_exp - 1, row_sems.at[0])
        take_all(land, n_exp - 1, row_sems.at[1])
        part = 4 * group
        for b in range(blocks):
            moved = jnp.dot(
                move_ref[...],
                land[pl.ds(b * group, group)].reshape(block, quarter),
                preferred_element_type=F32,
            ).astype(BF16)
            for q in range(4):
                flat[pl.ds(b * part, part), pl.ds(q * quarter, quarter)] = moved[
                    q * part : (q + 1) * part
                ]
        home = jnp.dot(taking_ref[...], flat[...], preferred_element_type=F32)
        tokens = token_ref.shape[0]
        token_ref[...] = (home[:tokens] + router_back).astype(BF16)
        routed_ref[...] = home[tokens:].astype(BF16)


def expert_rows(
    n_dp, n_exp, group, per_token, rows, move, unmove, router, mine, terms, slope, taking, gate, up, down
):
    hidden, width = gate.shape
    tile = 256
    slots = rows.shape[0] // 8
    tokens = slope.shape[0]

    def whole(array):
        return pl.BlockSpec(array.shape, lambda i: (0,) * len(array.shape))

    def out(*shape, kind=BF16):
        return jax.ShapeDtypeStruct(shape, kind)

    weight = pl.BlockSpec((tile, width), lambda i: (i, 0))
    outs = (
        out(taking.shape[0] - tokens, width),
        out(tokens, width),
        out(*terms.shape[1:], kind=F32),
        out(8, width, kind=F32),
    )
    wholes = (rows, move, unmove, router, mine, terms, slope, taking)
    message = pltpu.VMEM((slots // CAP, 16, width // 4), BF16)
    dma = pltpu.SemaphoreType.DMA
    return pl.pallas_call(
        functools.partial(expert_kernel, n_dp, n_exp, group, per_token),
        name="expert_rows",
        grid=(hidden // tile,),
        out_shape=outs,
        in_specs=[whole(array) for array in wholes] + [weight] * 3,
        out_specs=[whole(array) for array in outs],
        scratch_shapes=[
            pltpu.VMEM((slots, width), BF16),
            pltpu.VMEM((slots, width), BF16),
            pltpu.VMEM((slots, width), BF16),
            pltpu.VMEM((slots, 128), F32),
            pltpu.VMEM((slots, width), F32),
            pltpu.VMEM((slots, width), F32),
            message,
            message,
            pltpu.VMEM((2 * slots, width), BF16),
            pltpu.VMEM(terms.shape[1:], F32),
            pltpu.VMEM((n_dp, *terms.shape[1:]), F32),
            pltpu.VMEM((8, width), F32),
            pltpu.VMEM((n_dp, 8, width), F32),
            dma((2,)),
            dma((3,)),
            dma((2, n_dp)),
            dma((2, n_dp)),
        ],
        compiler_params=pltpu.CompilerParams(
            has_side_effects=True, vmem_limit_bytes=58 << 20
        ),
    )(*wholes, gate, up, down)


def on_device(n_dp, n_exp, tokens, routes, counts, router, gate_up_weight, down_weight, cotangent):
    members, tok_local = routes.shape
    width = tokens.shape[1]
    experts = router.shape[1]
    per_member = experts // members
    copies = members * tok_local
    tok_total = tok_local * n_dp * n_exp
    part = width // n_dp
    slots = experts * CAP
    d, mine = lax.axis_index("dp"), lax.axis_index("expert")

    earlier = (
        (routes[:, :, None] == routes[:, None, :])
        & (jnp.arange(tok_local)[None, None, :] < jnp.arange(tok_local)[None, :, None])
    ).astype(jnp.int32)
    rank = jnp.sum(earlier, axis=2)
    owners = routes + per_member * jnp.arange(members, dtype=jnp.int32)[:, None]
    group = min(16, experts)
    move_np = arrange(group)
    move, unmove = jnp.asarray(move_np, BF16), jnp.asarray(move_np.T, BF16)
    first = owners // group * (4 * group) + owners % group * CAP + rank
    second = first + 2 * group
    row_ids = jnp.arange(2 * slots, dtype=jnp.int32)
    token_hits = jnp.any(row_ids[:, None, None] == first[None, :, :], axis=1)
    copy_hits = row_ids[:, None] == second.reshape(1, copies)
    placing = jnp.concatenate([token_hits, copy_hits], axis=1).astype(BF16)
    token_takes = jnp.any(first[:, :, None] == row_ids[None, None, :], axis=0)
    copy_takes = second.reshape(copies, 1) == row_ids[None, :]
    taking = jnp.concatenate([token_takes, copy_takes], axis=0).astype(BF16)
    stacked = jnp.concatenate([tokens, cotangent.reshape(copies, width)], axis=0)
    held = jnp.pad(counts.astype(BF16), ((0, 0), (0, 256 - experts)))
    rows_in, terms_in, router_full, slope, gate_full, up_full, down_full = send_all(
        n_dp,
        n_exp,
        tok_local,
        placing,
        stacked,
        unmove,
        jnp.asarray(arrange_terms(group), BF16),
        jnp.broadcast_to(held, (group, 256)),
        router.reshape(2, part // 2, experts),
        gate_up_weight[0, :, 0, :],
        gate_up_weight[0, :, 1, :],
        down_weight[0],
    )

    is_mine = (jnp.arange(experts, dtype=jnp.int32) == mine).astype(F32)
    routed_out, token_grad, dense_sum, routed_sum = expert_rows(
        n_dp,
        n_exp,
        group,
        per_member / tok_total,
        rows_in.reshape(experts * 16, width // 4),
        move,
        unmove,
        router_full,
        jnp.broadcast_to(is_mine[None, :], (8, experts)),
        terms_in,
        slope,
        taking,
        gate_full.reshape(-1, width),
        up_full.reshape(-1, width),
        down_full.reshape(-1, width),
    )
    routed_out = routed_out.reshape(members, tok_local, width)
    load = dense_sum[width // 256, :experts]
    balance = per_member * jnp.sum(load * is_mine) / tok_total
    grad = BALANCE * balance * dense_sum.reshape(-1)[:width] + routed_sum[0]
    router_grad = lax.dynamic_slice(grad, (d * part,), (part,)) * tok_total ** (-0.5)
    return (routed_out, token_grad, router_grad[:, None])


def solution(mesh):
    in_specs = (
        P(("dp", "expert"), None),
        P(None, ("dp", "expert")),
        P(("dp", "expert"), None),
        P("dp", None),
        P("expert", "dp", None, None),
        P("expert", "dp", None),
        P(None, ("dp", "expert"), None),
    )
    out_specs = (P(None, ("dp", "expert"), None), P(("dp", "expert"), None), P("dp", "expert"))
    sizes = (mesh.shape["dp"], mesh.shape["expert"])
    return jax.shard_map(
        functools.partial(on_device, *sizes),
        mesh=mesh,
        in_specs=in_specs,
        out_specs=out_specs,
        check_vma=False,
    )
```

time: 258 us -> 250 us (0.969)
  blocking collectives: 11.5 us -> 0 us
  local copies, waits for them, and re-layouts: 10.2 us -> 18.2 us
  Pallas kernels: 228 us -> 224 us
  matrix products: 2.72 us -> 0 us
    all_gather x1 -> x0, blocking collectives: 11.5 us -> none  [on_device(): router_full = lax.all_gather(router, 'dp', axis=0, tiled=True)]
    unnamed x26 -> x28, local copies, waits for them, and re-layouts: 2.42 us -> 10.2 us
    pallas_call x4 -> x1, Pallas kernels: 108 us -> 103 us  [expert_rows(): pl.pallas_call(functools.partial(expert_kernel, n_dp, n_exp, group, per_t...]
    dot_general x2 -> x0, matrix products: 2.72 us -> none  [the longest x1 1.42 us: on_device(): logits = jnp.dot(tokens, router_full, preferred_element_type=F32)]
    slice x1, local copies, waits for them, and re-layouts: 2.8 us -> 5.39 us  [on_device(): gate_up_weight[0, :, 1, :]]
where the time goes in v3:
time: 250 us; the launch traced here: 249 us
  Pallas kernels  224 us (90%)
  local copies, waits for them, and re-layouts  18.2 us (7%)
  other arithmetic  5.34 us (2%)
    pallas_call x1, Pallas kernels, send_all(): pl.pallas_call(functools.partial(send_kernel, n_dp, n_exp), name='send_al...  121 us
    pallas_call x1, Pallas kernels, expert_rows(): pl.pallas_call(functools.partial(expert_kernel, n_dp, n_exp, group, per_t...  103 us
    unnamed x28, local copies, waits for them, and re-layouts  10.2 us
    slice x1, local copies, waits for them, and re-layouts, on_device(): gate_up_weight[0, :, 1, :]  5.39 us

profile of v3, /device:TPU:1, one launch (start us, length us, event | category | flops | bytes accessed | tf_op | source)
XLA Modules:
  0.0 249.3 jit_solution(6460842028622737442)
XLA Ops:
  0.6 1.0 convert_reduce_fusion
  1.6 0.8 broadcast_add_fusion
  2.4 0.1 eq.86
  2.5 0.1 iota_compare_fusion
  2.6 0.1 fusion
  2.7 0.2 copy.15
  2.9 0.2 add_convert_fusion.placing_ref
  3.1 5.4 %fusion.11 = (bf16[1,192,1,2560]{3,2,1,0:T(2,128)(2,1)S(1)}, bf16[1,192,1,2560]{3,2,1,0:T(2,128)(2,1)S(1)}) fusion(bf16[1,192,2,2560]{3,2,1,0:T(2,128)(2,1)} %param.14), kind=kLoop, calls=%fused_computation.35 | loop fusion | bytes 3932160 | tf_op jit(solution)/shard_map/slice | solution.py:546
  8.5 0.0 copy-start.9
  8.5 0.0 copy-start.10
  8.5 0.3 copy_bitcast_fusion
  8.8 0.0 copy-start.12
  8.8 0.0 copy-start.3
  8.8 0.0 copy-start.5
  8.8 0.0 copy-start.6
  8.8 0.0 copy-start.7
  8.8 0.9 copy-done.9
  9.7 0.0 copy-done.10
  9.7 0.1 pad_maximum_fusion.stacked_ref
  9.8 0.0 copy-done.12
  9.9 0.3 copy-done.3
  10.2 0.0 copy-done.5
  10.2 0.0 copy-done.6
  10.2 0.0 copy-done.7
  10.2 121.3 %send_all.1 = (bf16[128,16,640]{2,1,0:T(8,128)(2,1)S(1)}, bf16[128,16,256]{2,1,0:T(8,128)(2,1)S(1)}, bf16[2560,128]{1,0:T(8,128)(2,1)S(1)}, f32[48,128]{1,0:T(8,...) custom-call(bf16[512,240]{1,0:T(8,128)(2,1)S(1)} %add_convert_fusion.placi, ...), custom_call_target="tpu_custom_call" | custom-call | tf_op jit(solution)/shard_map/send_all/pallas_call | solution.py:225
  131.5 0.0 copy-start
  131.6 2.0 copy-done
  133.5 0.0 copy-start.1
  133.5 1.6 copy-done.1
  135.1 0.0 copy-start.2
  135.1 1.0 copy-done.2
  136.1 0.0 copy-start.4
  136.1 0.8 copy-done.4
  136.9 0.6 copy-done.8
  137.6 0.1 iota_compare_fusion.1
  137.7 0.1 fusion.1
  137.8 0.7 add_convert_fusion.1.taking_ref
  138.5 0.6 broadcast_in_dim.10.mine_ref
  139.1 102.9 %expert_rows.1 = (bf16[192,2560]{1,0:T(8,128)(2,1)}, bf16[48,2560]{1,0:T(8,128)(2,1)}, f32[16,256]{1,0:T(8,128)}, f32[8,2560]{1,0:T(8,128)}) custom-call(bf16[2048,640]{1,0:T(8,128)(2,1)} %bitcast.15, bf16[256,256]{1,0:T(8,128)(2,1)} %constant.69.clone.move_ref, bf16[256,256]{1,0:T(8,128)(2,1)} %constant.70.clone.unmove_ref, bf16[2560,128]{1,0:T(8,128)(2,1)} %copy-done.4, ...), custom_call_target="tpu_custom_call" | custom-call | tf_op jit(solution)/shard_map/expert_rows/pallas_call | solution.py:472
  242.1 0.0 copy-start.11
  242.1 1.3 fusion.9
  244.1 0.7 slice_multiply_fusion
  244.8 0.9 slice_reduce_fusion
  245.7 0.1 fusion.2
  245.8 0.6 broadcast_in_dim.11
  246.4 2.2 copy.24
  248.6 0.0 copy-done.11
  248.6 0.7 copy.25
  (8 shorter events, 0.1 us)
Async XLA Ops:
  8.5 1.2 copy-start.9
  8.5 1.2 copy-start.10
  8.8 1.0 copy-start.12
  8.8 1.4 copy-start.3
  8.8 1.4 copy-start.5
  8.8 1.4 copy-start.6
  8.8 1.4 copy-start.7
  131.5 2.0 copy-start
  133.5 1.6 copy-start.1
  135.1 1.0 copy-start.2
  136.1 0.8 copy-start.4
  136.9 0.6 copy-start.8
  242.1 6.5 %copy-start.11 = (bf16[48,2560]{1,0:T(8,128)(2,1)S(1)}, bf16[48,2560]{1,0:T(8,128)(2,1)}, u32[]{:S(2)}) copy-start(bf16[48,2560]{1,0:T(8,128)(2,1)} %get-tuple-element.35) | copy-start | bytes 737284

commit v4 on v3

v4 whole, which is shorter than its diff:
```python
import functools

import jax
import jax.numpy as jnp
import numpy as np
from jax import lax
from jax.experimental import pallas as pl
from jax.experimental.pallas import tpu as pltpu
from jax.sharding import PartitionSpec as P

ROUTE_SCALE = 2.5
BALANCE = 1.0
CAP = 2
STRIDE = 37
MESH = pl.DeviceIdType.MESH
BF16 = jnp.bfloat16
F32 = jnp.float32


def remote(src, dst, send_sem, recv_sem, device):
    return pltpu.make_async_remote_copy(
        src_ref=src,
        dst_ref=dst,
        send_sem=send_sem,
        recv_sem=recv_sem,
        device_id=device,
        device_id_type=MESH,
    )


def take_all(ref, count, sem):
    block = ref.at[pl.ds(0, count)]
    pltpu.make_async_copy(block, block, sem).wait()


def send_rows(n_exp, d, e, source, target, sems):
    def to_peer(s, carry):
        peer = (e + (s * STRIDE) % n_exp) % n_exp
        remote(source.at[peer], target.at[e], sems.at[0], sems.at[1], (d, peer)).start()
        return carry

    lax.fori_loop(1, n_exp, to_peer, 0)


def arrange(group):
    i = np.arange(group * 16)
    quarter, kind, expert, slot = i // (4 * group), i // (2 * group) % 2, i // 2 % group, i % 2
    move = np.zeros((group * 16, group * 16), np.float32)
    move[i, expert * 16 + quarter * 4 + kind * 2 + slot] = 1.0
    return move


def arrange_terms(group):
    i = np.arange(group * 16)
    move = np.zeros((group * 16, group * 16), np.float32)
    move[i, i % 16 * group + i // 16] = 1.0
    return move


def pack(first, second, unmove, quarter):
    parts = []
    for q in range(4):
        columns = slice(q * quarter, (q + 1) * quarter)
        parts += [first[:, columns], second[:, columns]]
    stacked = jnp.concatenate(parts, axis=0)
    return jnp.dot(unmove, stacked, preferred_element_type=F32).astype(BF16)


def layer_kernel(
    n_dp,
    n_exp,
    per_token,
    placing_ref,
    stacked_ref,
    move_ref,
    unmove_ref,
    unterm_ref,
    counts_ref,
    router_ref,
    mine_ref,
    gate_ref,
    up_ref,
    down_ref,
    routed_ref,
    token_ref,
    dense_ref,
    sum_ref,
    tok,
    cot,
    grad,
    value,
    total_out,
    total_grad,
    rows,
    rows_in,
    terms,
    terms_in,
    router_all,
    slope_s,
    gate_all,
    up_all,
    down_all,
    back,
    land,
    flat,
    dense_s,
    dense_land,
    lifted,
    lifted_land,
    row_sems,
    term_sems,
    self_sems,
    half_sems,
    swap_sems,
    own_send,
    own_recv,
    pass_send,
    pass_recv,
    back_sems,
    back_self,
    dense_sems,
    lifted_sems,
):
    d = lax.axis_index("dp")
    e = lax.axis_index("expert")
    core = e % 2
    sibling = e + 1 - 2 * core
    sides = ((d + 1) % n_dp, (d + n_dp - 1) % n_dp)
    span = gate_ref.shape[0] // 2
    held = (gate_ref, up_ref, down_ref)
    full = (gate_all, up_all, down_all)

    def piece(refs, shard, chunk):
        ref, part = refs[chunk // 2], pl.ds(chunk % 2 * span, span)
        return ref.at[part] if shard is None else ref.at[shard, part]

    orders = ((0, 1, 2, 3, 4, 5), (3, 4, 5, 0, 1, 2))

    def own(side, chunk):
        return remote(
            piece(held, None, chunk),
            piece(full, d, chunk),
            own_send.at[side, chunk],
            own_recv.at[side, chunk],
            (sides[side], e),
        )

    def passed(side, chunk):
        source = sides[1 - side]
        return remote(
            piece(full, source, chunk),
            piece(full, source, chunk),
            pass_send.at[side, chunk % 3],
            pass_recv.at[side, chunk % 3],
            (sides[side], e),
        )

    def router_half(step):
        return remote(
            router_ref.at[core],
            router_all.at[d, core],
            half_sems.at[0, step],
            half_sems.at[1, step],
            ((d + step) % n_dp, e),
        )

    def router_swap(step):
        shard = (d + n_dp - step) % n_dp
        return remote(
            router_all.at[shard, core],
            router_all.at[shard, core],
            swap_sems.at[0, step],
            swap_sems.at[1, step],
            (d, sibling),
        )

    for step in range(1, n_dp):
        router_half(step).start()
    for step in range(6):
        for side in range(2):
            own(side, orders[side][step]).start()
    own_router = pltpu.make_async_copy(router_ref, router_all.at[d], self_sems.at[5])
    own_router.start()
    locals_ = [
        pltpu.make_async_copy(gate_ref, gate_all.at[d], self_sems.at[0]),
        pltpu.make_async_copy(up_ref, up_all.at[d], self_sems.at[1]),
        pltpu.make_async_copy(down_ref, down_all.at[d], self_sems.at[2]),
    ]
    for copy in locals_:
        copy.start()

    group = unmove_ref.shape[0] // 16
    quarter = rows.shape[2]
    for b in range(n_exp // group):
        placed = jnp.dot(
            placing_ref[pl.ds(b * 4 * group, 4 * group), :],
            stacked_ref[...],
            preferred_element_type=F32,
        ).astype(BF16)
        rows[pl.ds(b * group, group)] = pack(
            placed[: 2 * group], placed[2 * group :], unmove_ref[...], quarter
        ).reshape(group, 16, quarter)
    send_rows(n_exp, d, e, rows, rows_in, row_sems)
    locals_.append(pltpu.make_async_copy(rows.at[e], rows_in.at[e], self_sems.at[3]))
    locals_[-1].start()

    for step in range(1, n_dp):
        router_half(step).wait_recv()
        router_swap(step).start()
    own_router.wait()
    for step in range(1, n_dp):
        router_swap(step).wait_recv()
    router = router_all[...].reshape(stacked_ref.shape[1], n_exp)
    tokens = stacked_ref[pl.ds(0, slope_s.shape[0]), :]
    affinity = jax.nn.sigmoid(jnp.dot(tokens, router, preferred_element_type=F32))
    slope = affinity * (1.0 - affinity)
    slope_s[...] = slope
    dense = lax.dot_general(
        slope.astype(BF16), tokens, (((0,), (0,)), ((), ())), preferred_element_type=F32
    ).astype(BF16)
    lanes = terms.shape[2]
    parts = tokens.shape[1] // lanes
    blank = jnp.zeros(((15 - parts) * group, lanes), BF16)
    for b in range(n_exp // group):
        block = [
            dense[b * group : (b + 1) * group, r * lanes : (r + 1) * lanes] for r in range(parts)
        ]
        stack = jnp.concatenate([*block, counts_ref[...], blank], axis=0)
        moved = jnp.dot(unterm_ref[...], stack, preferred_element_type=F32).astype(BF16)
        terms[pl.ds(b * group, group)] = moved.reshape(group, 16, lanes)
    send_rows(n_exp, d, e, terms, terms_in, term_sems)
    locals_.append(pltpu.make_async_copy(terms.at[e], terms_in.at[e], self_sems.at[4]))
    locals_[-1].start()

    for step in range(3):
        for side in range(2):
            chunk = orders[side][step]
            own(side, chunk).wait_recv()
            passed(side, chunk).start()

    transposed = (((1,), (1,)), ((), ()))
    block, part, two = 16 * group, 4 * group, 2 * group
    blocks = n_exp // group
    for copy in locals_:
        copy.wait()
    take_all(rows_in, n_exp - 1, row_sems.at[1])
    for b in range(blocks):
        moved = jnp.dot(
            move_ref[...],
            rows_in[pl.ds(b * group, group)].reshape(block, quarter),
            preferred_element_type=F32,
        ).astype(BF16)
        for q in range(4):
            at = (pl.ds(b * two, two), pl.ds(q * quarter, quarter))
            tok[at] = moved[2 * q * two : (2 * q + 1) * two]
            cot[at] = moved[(2 * q + 1) * two : (2 * q + 2) * two]
    logits = jnp.dot(tok[...], router, preferred_element_type=F32)
    gate = jax.nn.sigmoid(jnp.sum(logits * mine_ref[0:1, :], axis=1, keepdims=True))
    value[...] = jnp.broadcast_to(gate, value.shape)
    grad[...] = (ROUTE_SCALE * gate * cot[...].astype(F32)).astype(BF16)

    def expert_part(shard, first):
        gate_w, up_w, down_w = gate_all.at[shard], up_all.at[shard], down_all.at[shard]
        gate_pre = lax.dot_general(tok[...], gate_w[...], transposed, preferred_element_type=F32)
        up_pre = lax.dot_general(tok[...], up_w[...], transposed, preferred_element_type=F32)
        hidden_grad = lax.dot_general(
            grad[...], down_w[...], transposed, preferred_element_type=F32
        )
        squash = jax.nn.sigmoid(gate_pre)
        active = gate_pre * squash
        hidden = (active * up_pre).astype(BF16)
        gate_grad = (hidden_grad * up_pre * squash * (1.0 + gate_pre * (1.0 - squash))).astype(BF16)
        up_grad = (hidden_grad * active).astype(BF16)
        more_out = jnp.dot(hidden, down_w[...], preferred_element_type=F32)
        more_grad = jnp.dot(gate_grad, gate_w[...], preferred_element_type=F32) + jnp.dot(
            up_grad, up_w[...], preferred_element_type=F32
        )
        if first:
            total_out[...] = more_out
            total_grad[...] = more_grad
        else:
            total_out[...] += more_out
            total_grad[...] += more_grad

    expert_part(d, True)
    for side in range(2):
        for step in range(3, 6):
            own(side, orders[side][step]).wait_recv()
        expert_part(sides[1 - side], False)
    take_all(terms_in, n_exp - 1, term_sems.at[1])
    dense_s[...] = jnp.sum(terms_in[...].astype(F32), axis=0)
    for step in range(3):
        for side in range(2):
            passed(side, orders[side][step]).wait_recv()
    expert_part((d + 2) % n_dp, False)

    gate = value[:, 0:1]
    expert_out = total_out[...].astype(BF16).astype(F32)
    affinity_grad = ROUTE_SCALE * jnp.sum(
        cot[...].astype(F32) * expert_out, axis=1, keepdims=True
    )
    lift = gate * (1.0 - gate) * affinity_grad
    column = lax.dot_general(
        mine_ref[...].astype(BF16), router, transposed, preferred_element_type=F32
    )[0:1]
    lifted[...] = jnp.broadcast_to(
        jnp.sum(lift * tok[...].astype(F32), axis=0, keepdims=True), lifted.shape
    )

    def small(shift, ref, target, sems):
        return remote(
            ref,
            target.at[d],
            sems.at[0, shift],
            sems.at[1, shift],
            ((d + shift) % n_dp, e),
        )

    smalls = []
    for shift in range(1, n_dp):
        smalls.append(small(shift, dense_s, dense_land, dense_sems))
        smalls.append(small(shift, lifted, lifted_land, lifted_sems))
    for copy in smalls:
        copy.start()
    grad[...] = (total_grad[...] + lift * column).astype(BF16)
    tok[...] = (ROUTE_SCALE * gate * expert_out).astype(BF16)
    for b in range(blocks):
        at = pl.ds(b * two, two)
        back[pl.ds(b * group, group)] = pack(
            grad[at, :], tok[at, :], unmove_ref[...], quarter
        ).reshape(group, 16, quarter)
    send_rows(n_exp, d, e, back, land, back_sems)
    returns = (
        pltpu.make_async_copy(back.at[e], land.at[e], back_self.at[0]),
        pltpu.make_async_copy(dense_s, dense_land.at[d], back_self.at[1]),
        pltpu.make_async_copy(lifted, lifted_land.at[d], back_self.at[2]),
    )
    for copy in returns:
        copy.start()
    for copy in returns:
        copy.wait()
    for copy in smalls:
        copy.wait()
    sum_ref[...] = jnp.sum(lifted_land[...], axis=0)
    all_dense = jnp.sum(dense_land[...], axis=0)
    dense_ref[...] = all_dense
    parts = tok.shape[1] // all_dense.shape[1]
    load = all_dense[parts : parts + 1, : slope_s.shape[1]]
    spread = (slope_s[...] * (BALANCE * (per_token * load))).astype(BF16)
    router_back = lax.dot_general(
        spread, router, transposed, preferred_element_type=F32
    )

    take_all(back, n_exp - 1, back_sems.at[0])
    take_all(land, n_exp - 1, back_sems.at[1])
    for b in range(blocks):
        moved = jnp.dot(
            move_ref[...],
            land[pl.ds(b * group, group)].reshape(block, quarter),
            preferred_element_type=F32,
        ).astype(BF16)
        for q in range(4):
            flat[pl.ds(b * part, part), pl.ds(q * quarter, quarter)] = moved[
                q * part : (q + 1) * part
            ]
    home = lax.dot_general(
        placing_ref[...], flat[...], (((0,), (0,)), ((), ())), preferred_element_type=F32
    )
    count = token_ref.shape[0]
    token_ref[...] = (home[:count] + router_back).astype(BF16)
    routed_ref[...] = home[count:].astype(BF16)

    for step in range(1, n_dp):
        router_half(step).wait_send()
        router_swap(step).wait_send()
    for step in range(6):
        for side in range(2):
            own(side, orders[side][step]).wait_send()
    for step in range(3):
        for side in range(2):
            passed(side, orders[side][step]).wait_send()
    take_all(rows, n_exp - 1, row_sems.at[0])
    take_all(terms, n_exp - 1, term_sems.at[0])


def layer(n_dp, n_exp, tokens, per_token, wholes, weights):
    placing, stacked = wholes[:2]
    width = stacked.shape[1]
    slots = placing.shape[0] // 2
    hidden = weights[0].shape[0]

    def out(*shape, kind=BF16):
        return jax.ShapeDtypeStruct(shape, kind)

    def vmem(*shape, kind=BF16):
        return pltpu.VMEM(shape, kind)

    message = vmem(n_exp, 16, width // 4)
    terms = vmem(n_exp, 16, 256)
    gathered = vmem(n_dp, hidden, width)
    dma = pltpu.SemaphoreType.DMA
    return pl.pallas_call(
        functools.partial(layer_kernel, n_dp, n_exp, per_token),
        name="layer",
        out_shape=(
            out(stacked.shape[0] - tokens, width),
            out(tokens, width),
            out(16, 256, kind=F32),
            out(8, width, kind=F32),
        ),
        in_specs=[pl.BlockSpec(memory_space=pltpu.VMEM)] * 8
        + [pl.BlockSpec(memory_space=pl.ANY)] * 3,
        out_specs=[pl.BlockSpec(memory_space=pltpu.VMEM)] * 4,
        scratch_shapes=[
            *[vmem(slots, width)] * 3,
            vmem(slots, 128, kind=F32),
            *[vmem(slots, width, kind=F32)] * 2,
            *[message] * 2,
            *[terms] * 2,
            vmem(n_dp, *wholes[6].shape),
            vmem(tokens, n_exp, kind=F32),
            *[gathered] * 3,
            *[message] * 2,
            vmem(2 * slots, width),
            vmem(16, 256, kind=F32),
            vmem(n_dp, 16, 256, kind=F32),
            vmem(8, width, kind=F32),
            vmem(n_dp, 8, width, kind=F32),
            dma((2,)),
            dma((2,)),
            dma((6,)),
            dma((2, n_dp)),
            dma((2, n_dp)),
            dma((2, 6)),
            dma((2, 6)),
            dma((2, 3)),
            dma((2, 3)),
            dma((2,)),
            dma((3,)),
            dma((2, n_dp)),
            dma((2, n_dp)),
        ],
        compiler_params=pltpu.CompilerParams(
            has_side_effects=True, vmem_limit_bytes=60 << 20
        ),
    )(*wholes, *weights)


def on_device(n_dp, n_exp, tokens, routes, counts, router, gate_up_weight, down_weight, cotangent):
    members, tok_local = routes.shape
    width = tokens.shape[1]
    experts = router.shape[1]
    per_member = experts // members
    copies = members * tok_local
    tok_total = tok_local * n_dp * n_exp
    part = width // n_dp
    slots = experts * CAP
    d, mine = lax.axis_index("dp"), lax.axis_index("expert")

    earlier = (
        (routes[:, :, None] == routes[:, None, :])
        & (jnp.arange(tok_local)[None, None, :] < jnp.arange(tok_local)[None, :, None])
    ).astype(jnp.int32)
    rank = jnp.sum(earlier, axis=2)
    owners = routes + per_member * jnp.arange(members, dtype=jnp.int32)[:, None]
    group = min(16, experts)
    move_np = arrange(group)
    move, unmove = jnp.asarray(move_np, BF16), jnp.asarray(move_np.T, BF16)
    first = owners // group * (4 * group) + owners % group * CAP + rank
    second = first + 2 * group
    row_ids = jnp.arange(2 * slots, dtype=jnp.int32)
    token_hits = jnp.any(row_ids[:, None, None] == first[None, :, :], axis=1)
    copy_hits = row_ids[:, None] == second.reshape(1, copies)
    placing = jnp.concatenate([token_hits, copy_hits], axis=1).astype(BF16)
    stacked = jnp.concatenate([tokens, cotangent.reshape(copies, width)], axis=0)
    held = jnp.pad(counts.astype(BF16), ((0, 0), (0, 256 - experts)))
    is_mine = (jnp.arange(experts, dtype=jnp.int32) == mine).astype(F32)
    wholes = (
        placing,
        stacked,
        move,
        unmove,
        jnp.asarray(arrange_terms(group), BF16),
        jnp.broadcast_to(held, (group, 256)),
        router.reshape(2, part // 2, experts),
        jnp.broadcast_to(is_mine[None, :], (8, experts)),
    )
    weights = (gate_up_weight[0, :, 0, :], gate_up_weight[0, :, 1, :], down_weight[0])
    routed_out, token_grad, dense_sum, routed_sum = layer(
        n_dp, n_exp, tok_local, per_member / tok_total, wholes, weights
    )
    routed_out = routed_out.reshape(members, tok_local, width)
    load = dense_sum[width // 256, :experts]
    balance = per_member * jnp.sum(load * is_mine) / tok_total
    grad = BALANCE * balance * dense_sum.reshape(-1)[:width] + routed_sum[0]
    router_grad = lax.dynamic_slice(grad, (d * part,), (part,)) * tok_total ** (-0.5)
    return (routed_out, token_grad, router_grad[:, None])


def solution(mesh):
    in_specs = (
        P(("dp", "expert"), None),
        P(None, ("dp", "expert")),
        P(("dp", "expert"), None),
        P("dp", None),
        P("expert", "dp", None, None),
        P("expert", "dp", None),
        P(None, ("dp", "expert"), None),
    )
    out_specs = (P(None, ("dp", "expert"), None), P(("dp", "expert"), None), P("dp", "expert"))
    sizes = (mesh.shape["dp"], mesh.shape["expert"])
    return jax.shard_map(
        functools.partial(on_device, *sizes),
        mesh=mesh,
        in_specs=in_specs,
        out_specs=out_specs,
        check_vma=False,
    )
```

time: 250 us -> 217 us (0.87)
  Pallas kernels: 224 us -> 197 us
  local copies, waits for them, and re-layouts: 18.2 us -> 12.8 us
    pallas_call x2 -> x1, Pallas kernels: 224 us -> 197 us  [layer(): pl.pallas_call(functools.partial(layer_kernel, n_dp, n_exp, per_token), n...]
    unnamed x28 -> x12, local copies, waits for them, and re-layouts: 10.2 us -> 2.93 us
where the time goes in v4:
time: 217 us; the launch traced here: 216 us
  Pallas kernels  197 us (91%)
  local copies, waits for them, and re-layouts  12.8 us (6%)
  other arithmetic  4.68 us (2%)
    pallas_call x1, Pallas kernels, layer(): pl.pallas_call(functools.partial(layer_kernel, n_dp, n_exp, per_token), n...  197 us
    slice x1, local copies, waits for them, and re-layouts, on_device(): gate_up_weight[0, :, 1, :]  5.34 us

profile of v4, /device:TPU:1, one launch (start us, length us, event | category | flops | bytes accessed | tf_op | source)
XLA Modules:
  0.0 216.2 jit_solution(15117387230913596706)
XLA Ops:
  0.6 5.3 %fusion.10 = (bf16[1,192,1,2560]{3,2,1,0:T(2,128)(2,1)S(1)}, bf16[1,192,1,2560]{3,2,1,0:T(2,128)(2,1)S(1)}) fusion(bf16[1,192,2,2560]{3,2,1,0:T(2,128)(2,1)} %param.14), kind=kLoop, calls=%fused_computation.31 | loop fusion | bytes 3932160 | tf_op jit(solution)/shard_map/slice | solution.py:488
  6.0 0.0 copy-start.3
  6.0 0.0 copy-start
  6.0 0.0 copy-start.1
  6.0 1.6 copy_bitcast_fusion
  7.6 0.0 copy-start.4
  7.6 0.0 copy-done.3
  7.6 0.2 convert_reduce_fusion
  7.9 0.1 broadcast_add_fusion
  8.0 0.1 eq.60
  8.0 0.1 iota_compare_fusion
  8.1 0.1 fusion
  8.3 0.2 copy.15
  8.4 0.9 add_convert_fusion.placing_ref
  9.3 0.6 broadcast_in_dim.10.mine_ref
  9.9 0.0 copy-done
  9.9 0.0 copy-done.1
  9.9 1.1 pad_maximum_fusion.stacked_ref
  11.1 0.0 copy-done.4
  11.1 0.6 broadcast_in_dim.9.counts_ref
  11.7 197.3 %layer.1 = (bf16[192,2560]{1,0:T(8,128)(2,1)}, bf16[48,2560]{1,0:T(8,128)(2,1)}, f32[16,256]{1,0:T(8,128)}, f32[8,2560]{1,0:T(8,128)}) custom-call(bf16[512,240]{1,0:T(8,128)(2,1)} %add_convert_fusion.placing_ref, bf16[240,2560]{1,0:T(8,128)(2,1)} %pad_maximum_fusion.stacked_ref, bf16[256,256]{1,0:T(8,128)(2,1)} %constant.69.clone.move_ref, ...), custom_call_target="tpu_custom_call" | custom-call | tf_op jit(solution)/shard_map/layer/pallas_call | solution.py:402
  209.0 0.0 copy-start.2
  209.0 1.3 fusion.8
  211.0 0.7 slice_multiply_fusion
  211.7 0.9 slice_reduce_fusion
  212.6 0.1 fusion.1
  212.7 0.6 broadcast_in_dim.11
  213.3 2.2 %copy.24 = bf16[4,48,2560]{2,1,0:T(8,128)(2,1)} copy(bf16[4,48,2560]{2,1,0:T(8,128)(2,1)} %bitcast.12) | data formatting | bytes 1966080
  215.5 0.0 copy-done.2
  215.5 0.7 copy.25
  (6 shorter events, 0.0 us)
Async XLA Ops:
  6.0 1.7 copy-start.3
  6.0 3.9 %copy-start = (bf16[4,48,2560]{2,1,0:T(8,128)(2,1)S(1)}, bf16[4,48,2560]{2,1,0:T(8,128)(2,1)}, u32[]{:S(2)}) copy-start(bf16[4,48,2560]{2,1,0:T(8,128)(2,1)} %param.16) | copy-start | bytes 2949124
  6.0 3.9 %copy-start.1 = (bf16[48,2560]{1,0:T(8,128)(2,1)S(1)}, bf16[48,2560]{1,0:T(8,128)(2,1)}, u32[]{:S(2)}) copy-start(bf16[48,2560]{1,0:T(8,128)(2,1)} %param.10) | copy-start | bytes 737284
  7.6 3.4 %copy-start.4 = (s32[1,128]{1,0:T(1,128)S(1)}, s32[1,128]{1,0:T(1,128)}, u32[]{:S(2)}) copy-start(s32[1,128]{1,0:T(1,128)} %param.12) | copy-start | bytes 1540
  209.0 6.5 %copy-start.2 = (bf16[48,2560]{1,0:T(8,128)(2,1)S(1)}, bf16[48,2560]{1,0:T(8,128)(2,1)}, u32[]{:S(2)}) copy-start(bf16[48,2560]{1,0:T(8,128)(2,1)} %get-tuple-element.21) | copy-start | bytes 737284

commit v5 on v4

--- a/solution.py
+++ b/solution.py
@@ -70,21 +70,24 @@
     n_dp,
     n_exp,
     per_token,
-    placing_ref,
-    stacked_ref,
+    scale,
+    first_ref,
+    second_ref,
+    tokens_ref,
+    cotangent_ref,
     move_ref,
     unmove_ref,
     unterm_ref,
     counts_ref,
     router_ref,
-    mine_ref,
     gate_ref,
     up_ref,
     down_ref,
     routed_ref,
     token_ref,
-    dense_ref,
-    sum_ref,
+    router_grad_ref,
+    token_hits,
+    copy_hits,
     tok,
     cot,
     grad,
@@ -189,14 +192,23 @@
     for copy in locals_:
         copy.start()
 
+    first = first_ref[...]
+    row_ids = lax.broadcasted_iota(jnp.int32, token_hits.shape, 0)
+    hits = row_ids == first[0:1]
+    for m in range(1, first.shape[0]):
+        hits = hits | (row_ids == first[m : m + 1])
+    token_hits[...] = hits.astype(F32).astype(BF16)
+    row_ids = lax.broadcasted_iota(jnp.int32, copy_hits.shape, 0)
+    copy_hits[...] = (row_ids == second_ref[...]).astype(F32).astype(BF16)
+    is_mine = (lax.broadcasted_iota(jnp.int32, (8, n_exp), 1) == e).astype(F32)
+
     group = unmove_ref.shape[0] // 16
     quarter = rows.shape[2]
     for b in range(n_exp // group):
-        placed = jnp.dot(
-            placing_ref[pl.ds(b * 4 * group, 4 * group), :],
-            stacked_ref[...],
-            preferred_element_type=F32,
-        ).astype(BF16)
+        at = pl.ds(b * 4 * group, 4 * group)
+        placed = jnp.dot(token_hits[at, :], tokens_ref[...], preferred_element_type=F32)
+        placed += jnp.dot(copy_hits[at, :], cotangent_ref[...], preferred_element_type=F32)
+        placed = placed.astype(BF16)
         rows[pl.ds(b * group, group)] = pack(
             placed[: 2 * group], placed[2 * group :], unmove_ref[...], quarter
         ).reshape(group, 16, quarter)
@@ -210,8 +222,8 @@
     own_router.wait()
     for step in range(1, n_dp):
         router_swap(step).wait_recv()
-    router = router_all[...].reshape(stacked_ref.shape[1], n_exp)
-    tokens = stacked_ref[pl.ds(0, slope_s.shape[0]), :]
+    router = router_all[...].reshape(tokens_ref.shape[1], n_exp)
+    tokens = tokens_ref[...]
     affinity = jax.nn.sigmoid(jnp.dot(tokens, router, preferred_element_type=F32))
     slope = affinity * (1.0 - affinity)
     slope_s[...] = slope
@@ -220,12 +232,19 @@
     ).astype(BF16)
     lanes = terms.shape[2]
     parts = tokens.shape[1] // lanes
+    held_counts = jnp.concatenate(
+        [
+            jnp.broadcast_to(counts_ref[...].astype(F32), (group, n_exp)),
+            jnp.zeros((group, lanes - n_exp), F32),
+        ],
+        axis=1,
+    ).astype(BF16)
     blank = jnp.zeros(((15 - parts) * group, lanes), BF16)
     for b in range(n_exp // group):
         block = [
             dense[b * group : (b + 1) * group, r * lanes : (r + 1) * lanes] for r in range(parts)
         ]
-        stack = jnp.concatenate([*block, counts_ref[...], blank], axis=0)
+        stack = jnp.concatenate([*block, held_counts, blank], axis=0)
         moved = jnp.dot(unterm_ref[...], stack, preferred_element_type=F32).astype(BF16)
         terms[pl.ds(b * group, group)] = moved.reshape(group, 16, lanes)
     send_rows(n_exp, d, e, terms, terms_in, term_sems)
@@ -255,7 +274,7 @@
             tok[at] = moved[2 * q * two : (2 * q + 1) * two]
             cot[at] = moved[(2 * q + 1) * two : (2 * q + 2) * two]
     logits = jnp.dot(tok[...], router, preferred_element_type=F32)
-    gate = jax.nn.sigmoid(jnp.sum(logits * mine_ref[0:1, :], axis=1, keepdims=True))
+    gate = jax.nn.sigmoid(jnp.sum(logits * is_mine[0:1, :], axis=1, keepdims=True))
     value[...] = jnp.broadcast_to(gate, value.shape)
     grad[...] = (ROUTE_SCALE * gate * cot[...].astype(F32)).astype(BF16)
 
@@ -301,7 +320,7 @@
     )
     lift = gate * (1.0 - gate) * affinity_grad
     column = lax.dot_general(
-        mine_ref[...].astype(BF16), router, transposed, preferred_element_type=F32
+        is_mine.astype(BF16), router, transposed, preferred_element_type=F32
     )[0:1]
     lifted[...] = jnp.broadcast_to(
         jnp.sum(lift * tok[...].astype(F32), axis=0, keepdims=True), lifted.shape
@@ -341,11 +360,20 @@
         copy.wait()
     for copy in smalls:
         copy.wait()
-    sum_ref[...] = jnp.sum(lifted_land[...], axis=0)
     all_dense = jnp.sum(dense_land[...], axis=0)
-    dense_ref[...] = all_dense
-    parts = tok.shape[1] // all_dense.shape[1]
-    load = all_dense[parts : parts + 1, : slope_s.shape[1]]
+    all_lifted = jnp.sum(lifted_land[...], axis=0)[0:1]
+    pieces = tok.shape[1] // all_dense.shape[1]
+    load = all_dense[pieces : pieces + 1, :n_exp]
+    my_load = jnp.sum(load * is_mine[0:1], axis=1, keepdims=True)
+    dense_row = jnp.concatenate([all_dense[r : r + 1] for r in range(pieces)], axis=1)
+    router_terms = (BALANCE * (per_token * my_load) * dense_row + all_lifted) * scale
+    share = router_grad_ref.shape[1]
+    for p in range(n_dp):
+
+        @pl.when(d == p)
+        def _(p=p):
+            router_grad_ref[...] = router_terms[:, p * share : (p + 1) * share]
+
     spread = (slope_s[...] * (BALANCE * (per_token * load))).astype(BF16)
     router_back = lax.dot_general(
         spread, router, transposed, preferred_element_type=F32
@@ -363,12 +391,12 @@
             flat[pl.ds(b * part, part), pl.ds(q * quarter, quarter)] = moved[
                 q * part : (q + 1) * part
             ]
-    home = lax.dot_general(
-        placing_ref[...], flat[...], (((0,), (0,)), ((), ())), preferred_element_type=F32
-    )
-    count = token_ref.shape[0]
-    token_ref[...] = (home[:count] + router_back).astype(BF16)
-    routed_ref[...] = home[count:].astype(BF16)
+    over_rows = (((0,), (0,)), ((), ()))
+    home = lax.dot_general(token_hits[...], flat[...], over_rows, preferred_element_type=F32)
+    token_ref[...] = (home + router_back).astype(BF16)
+    routed_ref[...] = lax.dot_general(
+        copy_hits[...], flat[...], over_rows, preferred_element_type=F32
+    ).astype(BF16)
 
     for step in range(1, n_dp):
         router_half(step).wait_send()
@@ -383,10 +411,10 @@
     take_all(terms, n_exp - 1, term_sems.at[0])
 
 
-def layer(n_dp, n_exp, tokens, per_token, wholes, weights):
-    placing, stacked = wholes[:2]
-    width = stacked.shape[1]
-    slots = placing.shape[0] // 2
+def layer(n_dp, n_exp, per_token, scale, wholes, weights):
+    own, cotangent = wholes[2:4]
+    tokens, width = own.shape
+    slots = n_exp * CAP
     hidden = weights[0].shape[0]
 
     def out(*shape, kind=BF16):
@@ -400,24 +428,25 @@
     gathered = vmem(n_dp, hidden, width)
     dma = pltpu.SemaphoreType.DMA
     return pl.pallas_call(
-        functools.partial(layer_kernel, n_dp, n_exp, per_token),
+        functools.partial(layer_kernel, n_dp, n_exp, per_token, scale),
         name="layer",
         out_shape=(
-            out(stacked.shape[0] - tokens, width),
+            out(*cotangent.shape),
             out(tokens, width),
-            out(16, 256, kind=F32),
-            out(8, width, kind=F32),
+            out(1, width // n_dp, kind=F32),
         ),
-        in_specs=[pl.BlockSpec(memory_space=pltpu.VMEM)] * 8
+        in_specs=[pl.BlockSpec(memory_space=pltpu.VMEM)] * 9
         + [pl.BlockSpec(memory_space=pl.ANY)] * 3,
-        out_specs=[pl.BlockSpec(memory_space=pltpu.VMEM)] * 4,
+        out_specs=[pl.BlockSpec(memory_space=pltpu.VMEM)] * 3,
         scratch_shapes=[
+            vmem(2 * slots, tokens),
+            vmem(2 * slots, cotangent.shape[0]),
             *[vmem(slots, width)] * 3,
             vmem(slots, 128, kind=F32),
             *[vmem(slots, width, kind=F32)] * 2,
             *[message] * 2,
             *[terms] * 2,
-            vmem(n_dp, *wholes[6].shape),
+            vmem(n_dp, *wholes[8].shape),
             vmem(tokens, n_exp, kind=F32),
             *[gathered] * 3,
             *[message] * 2,
@@ -454,8 +483,6 @@
     copies = members * tok_local
     tok_total = tok_local * n_dp * n_exp
     part = width // n_dp
-    slots = experts * CAP
-    d, mine = lax.axis_index("dp"), lax.axis_index("expert")
 
     earlier = (
         (routes[:, :, None] == routes[:, None, :])
@@ -468,33 +495,23 @@
     move, unmove = jnp.asarray(move_np, BF16), jnp.asarray(move_np.T, BF16)
     first = owners // group * (4 * group) + owners % group * CAP + rank
     second = first + 2 * group
-    row_ids = jnp.arange(2 * slots, dtype=jnp.int32)
-    token_hits = jnp.any(row_ids[:, None, None] == first[None, :, :], axis=1)
-    copy_hits = row_ids[:, None] == second.reshape(1, copies)
-    placing = jnp.concatenate([token_hits, copy_hits], axis=1).astype(BF16)
-    stacked = jnp.concatenate([tokens, cotangent.reshape(copies, width)], axis=0)
-    held = jnp.pad(counts.astype(BF16), ((0, 0), (0, 256 - experts)))
-    is_mine = (jnp.arange(experts, dtype=jnp.int32) == mine).astype(F32)
     wholes = (
-        placing,
-        stacked,
+        first,
+        second.reshape(1, copies),
+        tokens,
+        cotangent.reshape(copies, width),
         move,
         unmove,
         jnp.asarray(arrange_terms(group), BF16),
-        jnp.broadcast_to(held, (group, 256)),
+        counts,
         router.reshape(2, part // 2, experts),
-        jnp.broadcast_to(is_mine[None, :], (8, experts)),
     )
     weights = (gate_up_weight[0, :, 0, :], gate_up_weight[0, :, 1, :], down_weight[0])
-    routed_out, token_grad, dense_sum, routed_sum = layer(
-        n_dp, n_exp, tok_local, per_member / tok_total, wholes, weights
+    routed_out, token_grad, router_grad = layer(
+        n_dp, n_exp, per_member / tok_total, tok_total ** (-0.5), wholes, weights
     )
     routed_out = routed_out.reshape(members, tok_local, width)
-    load = dense_sum[width // 256, :experts]
-    balance = per_member * jnp.sum(load * is_mine) / tok_total
-    grad = BALANCE * balance * dense_sum.reshape(-1)[:width] + routed_sum[0]
-    router_grad = lax.dynamic_slice(grad, (d * part,), (part,)) * tok_total ** (-0.5)
-    return (routed_out, token_grad, router_grad[:, None])
+    return (routed_out, token_grad, router_grad.reshape(part, 1))
 
 
 def solution(mesh):

time: 217 us -> 210 us (0.968)
  other arithmetic: 4.68 us -> 0.9 us
where the time goes in v5:
time: 210 us
  Pallas kernels  198 us (94%)
  local copies, waits for them, and re-layouts  11.1 us (5%)
    pallas_call x1, Pallas kernels, layer(): pl.pallas_call(functools.partial(layer_kernel, n_dp, n_exp, per_token, sc...  198 us
    slice x1, local copies, waits for them, and re-layouts, on_device(): gate_up_weight[0, :, 1, :]  5.34 us

profile of v5, /device:TPU:1, one launch (start us, length us, event | category | flops | bytes accessed | tf_op | source)
XLA Modules:
  0.0 210.2 jit_solution(8777440026524204745)
XLA Ops:
  0.6 5.3 %fusion.7 = (bf16[1,192,1,2560]{3,2,1,0:T(2,128)(2,1)S(1)}, bf16[1,192,1,2560]{3,2,1,0:T(2,128)(2,1)S(1)}) fusion(bf16[1,192,2,2560]{3,2,1,0:T(2,128)(2,1)} %param.14), kind=kLoop, calls=%fused_computation.18 | loop fusion | bytes 3932160 | tf_op jit(solution)/shard_map/slice | solution.py:509
  6.0 0.0 copy-start.1
  6.0 1.5 copy_bitcast_fusion
  7.5 0.0 copy-done.1
  7.6 0.2 convert_reduce_fusion
  7.8 0.7 broadcast_add_fusion
  8.4 0.6 reshape.43.second_ref
  9.1 197.6 %layer.1 = (bf16[192,2560]{1,0:T(8,128)(2,1)}, bf16[48,2560]{1,0:T(8,128)(2,1)}, f32[1,640]{1,0:T(1,128)}) custom-call(s32[4,48]{1,0:T(4,128)} %get-tuple-element.10.first_ref, s32[1,192]{1,0:T(1,128)} %reshape.43.second_ref, bf16[48,2560]{1,0:T(8,128)(2,1)} %tokens_ref.1, bf16[192,2560]{1,0:T(8,128)(2,1)} %bitcast.9, ...), custom_call_target="tpu_custom_call" | custom-call | tf_op jit(solution)/shard_map/layer/pallas_call | solution.py:430
  206.7 0.0 copy-start
  206.7 0.0 copy-start.2
  206.7 2.2 %copy.24 = bf16[4,48,2560]{2,1,0:T(8,128)(2,1)} copy(bf16[4,48,2560]{2,1,0:T(8,128)(2,1)} %bitcast.11) | data formatting | bytes 1966080
  209.0 0.0 copy-done
  209.0 0.7 copy.25
  209.7 0.0 copy-done.2
  209.7 0.6 copy.26
  (2 shorter events, 0.0 us)
Async XLA Ops:
  6.0 1.6 copy-start.1
  206.7 2.3 %copy-start = (bf16[48,2560]{1,0:T(8,128)(2,1)S(1)}, bf16[48,2560]{1,0:T(8,128)(2,1)}, u32[]{:S(2)}) copy-start(bf16[48,2560]{1,0:T(8,128)(2,1)} %get-tuple-element.19) | copy-start | bytes 737284
  206.7 3.0 %copy-start.2 = (f32[1,640]{1,0:T(1,128)S(1)}, f32[1,640]{1,0:T(1,128)}, u32[]{:S(2)}) copy-start(f32[1,640]{1,0:T(1,128)} %get-tuple-element.8) | copy-start | bytes 7684
